TPU v7x, 32 devices: a whole 2x2x4 slice. The times are simulated.
32 devices in a mesh: series: 8 (over y, x, core), tm: 4 (over z).
Axes of the slice: x: 2, y: 2, z: 4, core: 2. Of those that a mesh axis runs over, the one named last changes fastest.
Arguments:
- metric: bfloat16 [8192, 4096], P('series', 'tm'), may hold values from -6 to 6
- omega: bfloat16 [4096, 256], P('tm'), may hold values from -0.09375 to 0.09375
- psi: bfloat16 [513, 8192], P(None, 'series'), may hold values from -0.0625 to 0.0625
- phi: bfloat16 [512, 8192], P(None, 'series'), may hold values from -0.0625 to 0.0625
- theta: bfloat16 [512, 4096], P(None, 'tm'), may hold values from -0.09375 to 0.09375
- range_old: float32 [8192, 256], P('series', 'tm'), may hold values from -6 to 6
- corange_old: float32 [513, 4096], P(None, ('tm', 'series')), may hold values from -6 to 6
- core_old: float32 [512, 512], replicated, may hold values from -6 to 6
Outputs:
- range_new: float32 [8192, 256], P('series', 'tm')
- corange_new: float32 [513, 4096], P(None, ('tm', 'series'))
- core_new: float32 [512, 512], replicated
All inputs are finite; a program needn't handle non-finite values.
Results may differ from a plain program's by a relative error of at most 0.0003.
Values sent between devices are 32-bit elements; how exact they have to be, the bound alone decides.
No kernel may reach another device: no remote copies, remote signals or barrier semaphores. Data moves between devices by JAX's collectives and lax.ppermute only.
A program may use at most 64 MiB of HBM per device.

v0:
```python
import jax
import jax.numpy as jnp
from jax import lax
from jax.sharding import PartitionSpec as P


def body(metric, omega, psi, phi, theta, range_old, corange_old, core_old):
    range_term = jnp.dot(metric, omega, preferred_element_type=jnp.float32)
    range_sum = lax.psum_scatter(range_term, "tm", scatter_dimension=1, tiled=True)
    range_new = range_old + range_sum
    corange_term = jnp.dot(psi, metric, preferred_element_type=jnp.float32)
    left_term = jnp.dot(phi, metric, preferred_element_type=jnp.float32)
    corange_sum = lax.psum_scatter(corange_term, "series", scatter_dimension=1, tiled=True)
    core_term = jnp.einsum(
        "sc,tc->st", left_term, theta.astype(jnp.float32), precision=lax.Precision.HIGHEST
    )
    core_sum = lax.psum(core_term, ("series", "tm"))
    corange_new = corange_old + corange_sum
    core_new = core_old + core_sum
    return (range_new, corange_new, core_new)


def solution(mesh):
    return jax.shard_map(
        body,
        mesh=mesh,
        in_specs=(
            P("series", "tm"),
            P("tm", None),
            P(None, "series"),
            P(None, "series"),
            P(None, "tm"),
            P("series", "tm"),
            P(None, ("tm", "series")),
            P(),
        ),
        out_specs=(P("series", "tm"), P(None, ("tm", "series")), P()),
        check_vma=False,
    )
```

profile of v0, /device:TPU:0, one launch (start us, length us, event | category | flops | bytes accessed | tf_op | source)
XLA Modules:
  0.0 172.1 jit_solution(9763438258314023506)
XLA Ops:
  8.0 0.0 copy-start
  8.0 0.0 copy-start.2
  8.0 0.0 all-reduce.2.cloned.1.call-start
  8.1 1.5 copy-done
  9.6 2.5 %fusion.2 = f32[512,1024]{1,0:T(8,128)S(1)} fusion(bf16[512,1024]{1,0:T(8,128)(2,1)} %param.11, bf16[1024,1024]{1,0:T(8,128)(2,1)S(1)} %copy-done), kind=kOutput, calls=%fused_computation.2 | convolution fusion | flops 1073741824 | bytes 5242880 | tf_op jit(solution)/shard_map/dot_general | solution.py:12
  12.1 0.0 copy-done.2
  12.1 2.8 %fusion.3 = f32[512,512]{1,0:T(8,128)} fusion(f32[512,1024]{1,0:T(8,128)S(1)} %fusion.2, bf16[512,1024]{1,0:T(8,128)(2,1)S(1)} %copy-done.2), kind=kOutput, calls=%fused_computation.3 | convolution fusion | flops 3221225472 | bytes 4194304 | tf_op jit(solution)/shard_map/sc,tc->st/dot_general | solution.py:14
  14.9 0.0 all-reduce.2.cloned.1.call-update
  14.9 0.0 copy-start.4
  14.9 0.0 reduce-scatter.3.cloned.1.call-start
  15.0 2.9 %fusion = f32[1024,256]{0,1:T(8,128)} fusion(bf16[1024,1024]{1,0:T(8,128)(2,1)S(1)} %copy-done, bf16[1024,256]{1,0:T(8,128)(2,1)} %param.9), kind=kOutput, calls=%fused_computation | convolution fusion | flops 536870912 | bytes 3670016 | tf_op jit(solution)/shard_map/dot_general | solution.py:8
  17.9 0.0 reduce-scatter.3.cloned.1.call-update
  17.9 0.0 reduce-scatter.5.cloned.1.call-start
  17.9 0.0 copy-done.4
  17.9 2.6 %fusion.1 = f32[513,1024]{1,0:T(8,128)} fusion(bf16[513,1024]{1,0:T(8,128)(2,1)S(1)} %copy-done.4, bf16[1024,1024]{1,0:T(8,128)(2,1)S(1)} %copy-done), kind=kOutput, calls=%fused_computation.1 | convolution fusion | flops 1075838976 | bytes 5249024 | tf_op jit(solution)/shard_map/dot_general | solution.py:11
  20.6 0.0 copy-start.1
  20.6 0.0 reduce-scatter.5.cloned.1.call-update
  20.6 0.0 copy-start.3
  20.6 138.2 %all-reduce.2.cloned.1.call-done = f32[512,512]{1,0:T(8,128)} async-done(((f32[512,512]{1,0:T(8,128)}), f32[512,512]{1,0:T(8,128)}) %all-reduce.2.cloned.1.call-update) | async-done | bytes 1048592 | tf_op jit(solution)/shard_map/psum | solution.py:17
  158.8 0.0 copy-done.1
  158.8 2.4 %add.17 = f32[512,512]{1,0:T(8,128)} add(f32[512,512]{1,0:T(8,128)S(1)} %copy-done.1, f32[512,512]{1,0:T(8,128)} %all-reduce.2.cloned.1.call-done) | non-fusion elementwise | flops 262144 | bytes 3145728 | tf_op jit(solution)/shard_map/add | solution.py:19
  161.2 0.0 reduce-scatter.3.cloned.1.call-done
  161.2 1.8 %add.15 = f32[1024,64]{0,1:T(8,128)} add(f32[1024,64]{0,1:T(8,128)} %param.13, f32[1024,64]{0,1:T(8,128)} %reduce-scatter.3.cloned.1.call-done) | non-fusion elementwise | flops 65536 | bytes 786432 | tf_op jit(solution)/shard_map/add | solution.py:10
  163.0 0.0 reduce-scatter.5.cloned.1.call-done
  163.0 0.0 copy-done.3
  163.0 1.7 add.16
Async XLA Ops:
  8.0 1.6 copy-start
  8.0 4.1 %copy-start.2 = (bf16[512,1024]{1,0:T(8,128)(2,1)S(1)}, bf16[512,1024]{1,0:T(8,128)(2,1)}, u32[]{:S(2)}) copy-start(bf16[512,1024]{1,0:T(8,128)(2,1)} %param.12) | copy-start | bytes 3145732
  8.0 150.8 %all-reduce.2.cloned.1.call-start = ((), (), s32[]{:S(2)}) async-start(), calls=%async_computation.4 | async-start | bytes 2097152 | tf_op jit(solution)/shard_map/psum | solution.py:17
  14.9 3.0 %copy-start.4 = (bf16[513,1024]{1,0:T(8,128)(2,1)S(1)}, bf16[513,1024]{1,0:T(8,128)(2,1)}, u32[]{:S(2)}) copy-start(bf16[513,1024]{1,0:T(8,128)(2,1)} %param.10) | copy-start | bytes 3151876
  14.9 146.3 %reduce-scatter.3.cloned.1.call-start = ((), (), s32[]{:S(2)}) async-start(), calls=%async_computation.2 | async-start | bytes 1310720 | tf_op jit(solution)/shard_map/reduce_scatter | solution.py:9
  17.9 145.1 %reduce-scatter.5.cloned.1.call-start = ((), (), s32[]{:S(2)}) async-start(), calls=%async_computation.3 | async-start | bytes 2396160 | tf_op jit(solution)/shard_map/reduce_scatter | solution.py:13
  20.6 138.2 %copy-start.1 = (f32[512,512]{1,0:T(8,128)S(1)}, f32[512,512]{1,0:T(8,128)}, u32[]{:S(2)}) copy-start(f32[512,512]{1,0:T(8,128)} %param.15) | copy-start | bytes 3145732
  20.6 142.4 %copy-start.3 = (f32[513,128]{1,0:T(8,128)S(1)}, f32[513,128]{1,0:T(8,128)}, u32[]{:S(2)}) copy-start(f32[513,128]{1,0:T(8,128)} %param.14) | copy-start | bytes 787972
Sparse Core Ops, SparseCore 0:
  15.0 143.7 all-reduce.1
Sparse Core Ops, SparseCore 1:
  18.0 31.6 reduce-scatter.2
  53.3 40.3 reduce-scatter.4
where the time goes:
time: 172 us
  waiting for transfers between devices  138 us (80%)
  between operations  15.5 us (9%)
  matrix products  10.8 us (6%)
  other arithmetic  5.84 us (3%)
    psum x1, waiting for transfers between devices, body(): core_sum = lax.psum(core_term, ('series', 'tm'))  138 us
  transfers between devices with their start and end apart: 3, of which 1 were waited for; matrix products, arithmetic and copies ran while one was open for 6% of the time, Pallas kernels for 0%

commit v1 on v0

v1 whole, which is shorter than its diff:
```python
import functools
import operator

import jax
import jax.numpy as jnp
from jax import lax
from jax.experimental import pallas as pl
from jax.experimental.pallas import tpu as pltpu
from jax.sharding import PartitionSpec as P

F32 = jnp.float32
RADIX = 4
VMEM_LIMIT = 48 * 1024 * 1024


def added(terms):
    return functools.reduce(operator.add, terms)


def swap(value, axis, bits, size):
    return lax.ppermute(value, axis, [(i, i ^ bits) for i in range(size)])


def params():
    return pltpu.CompilerParams(vmem_limit_bytes=VMEM_LIMIT)


def whole(shape):
    return pl.BlockSpec(shape, lambda i, at: (0,) * len(shape))


def core_kernel(parts, at_ref, phi_ref, metric_ref, theta_ref, out_ref, sum_ref):
    chip = at_ref[1]
    left = jnp.dot(phi_ref[...], metric_ref[...], preferred_element_type=F32)
    high = left.astype(jnp.bfloat16)
    low = (left - high.astype(F32)).astype(jnp.bfloat16)
    theta = theta_ref[...]
    by_rows = (((1,), (1,)), ((), ()))
    sum_ref[...] = lax.dot_general(high, theta, by_rows, preferred_element_type=F32)
    sum_ref[...] += lax.dot_general(low, theta, by_rows, preferred_element_type=F32)
    rows = sum_ref.shape[0] // parts
    for k in range(parts):
        first = pl.multiple_of((chip ^ k) * rows, rows)
        out_ref[k] = sum_ref[pl.ds(first, rows), :]


def core_half(half, chip, phi, metric, theta, parts):
    order, depth = phi.shape
    rows = order // 2
    cols = theta.shape[0]
    return pl.pallas_call(
        functools.partial(core_kernel, parts),
        grid_spec=pltpu.PrefetchScalarGridSpec(
            num_scalar_prefetch=1,
            grid=(1,),
            in_specs=[
                pl.BlockSpec((rows, depth), lambda i, at: (at[0], 0)),
                whole(metric.shape),
                whole(theta.shape),
            ],
            out_specs=whole((parts, rows // parts, cols)),
            scratch_shapes=[pltpu.VMEM((rows, cols), F32)],
        ),
        out_shape=jax.ShapeDtypeStruct((parts, rows // parts, cols), F32),
        compiler_params=params(),
        name="core_half",
    )(jnp.stack([half, chip]), phi, metric, theta)


def range_kernel(parts, at_ref, omega_ref, metric_ref, send_ref, far_ref, own_ref, sum_ref):
    slot = at_ref[0]
    sum_ref[...] = lax.dot_general(
        omega_ref[...], metric_ref[...], (((0,), (1,)), ((), ())), preferred_element_type=F32
    )
    rows = sum_ref.shape[0] // parts

    def block(k):
        return sum_ref[pl.ds(pl.multiple_of((slot ^ k) * rows, rows), rows), :]

    for j in range(parts // 2):
        send_ref[j] = block(2 * j + 1)
    for j in range(1, parts // 2):
        far_ref[j - 1] = block(2 * j)
    own_ref[...] = block(0)


def range_blocks(slot, omega, metric, parts):
    series, width = metric.shape[0], omega.shape[1]
    rows = width // parts
    shapes = [(parts // 2, rows, series), (parts // 2 - 1, rows, series), (rows, series)]
    return pl.pallas_call(
        functools.partial(range_kernel, parts),
        grid_spec=pltpu.PrefetchScalarGridSpec(
            num_scalar_prefetch=1,
            grid=(1,),
            in_specs=[whole(omega.shape), whole(metric.shape)],
            out_specs=[whole(s) for s in shapes],
            scratch_shapes=[pltpu.VMEM((width, series), F32)],
        ),
        out_shape=[jax.ShapeDtypeStruct(s, F32) for s in shapes],
        compiler_params=params(),
        name="range_blocks",
    )(jnp.stack([slot]), omega, metric)


def corange_kernel(at_ref, psi_ref, metric_ref, send_ref, keep_ref, sum_ref):
    core = at_ref[1]
    sum_ref[...] = jnp.dot(psi_ref[...], metric_ref[...], preferred_element_type=F32)
    cols = keep_ref.shape[2]
    keep_ref[0] = sum_ref[:, pl.ds(pl.multiple_of(core * cols, cols), cols)]
    send_ref[0] = sum_ref[:, pl.ds(pl.multiple_of((1 - core) * cols, cols), cols)]


def corange_blocks(core, chip, psi, metric, parts):
    rows, depth = psi.shape
    cols = metric.shape[1] // (2 * parts)
    if cols % 128:
        term = jnp.dot(psi, metric, preferred_element_type=F32).reshape(rows, parts, 2, cols)
        term = jnp.take(term, chip ^ jnp.arange(parts), axis=1)
        pick = lambda c: lax.dynamic_index_in_dim(term, c, 2, keepdims=False).transpose(1, 0, 2)
        return pick(1 - core), pick(core)
    shape = jax.ShapeDtypeStruct((parts, rows, cols), F32)
    block = pl.BlockSpec((1, rows, cols), lambda k, at: (k, 0, 0))
    return pl.pallas_call(
        corange_kernel,
        grid_spec=pltpu.PrefetchScalarGridSpec(
            num_scalar_prefetch=1,
            grid=(parts,),
            in_specs=[
                whole(psi.shape),
                pl.BlockSpec((depth, 2 * cols), lambda k, at: (0, at[0] ^ k)),
            ],
            out_specs=[block, block],
            scratch_shapes=[pltpu.VMEM((rows, 2 * cols), F32)],
        ),
        out_shape=[shape, shape],
        compiler_params=params(),
        name="corange_blocks",
    )(jnp.stack([chip, core]), psi, metric)


def place_kernel(rows, half, radix, at_ref, old_ref, *refs):
    core, chip = at_ref[0], at_ref[1]
    pieces, out_ref = refs[:-1], refs[-1]
    for i, ref in enumerate(pieces):
        side, digit = i // radix, i % radix
        for g in range(ref.shape[0]):
            row = ((core ^ side) * half + (chip ^ (g * radix + digit))) * rows
            at = pl.ds(pl.multiple_of(row, rows), rows)
            out_ref[at, :] = old_ref[at, :] + ref[g]


def placed(core, chip, old, pieces, parts):
    rows = old.shape[0] // (2 * parts)
    return pl.pallas_call(
        functools.partial(place_kernel, rows, parts, len(pieces) // 2),
        grid_spec=pltpu.PrefetchScalarGridSpec(
            num_scalar_prefetch=1,
            grid=(1,),
            in_specs=[whole(old.shape)] + [whole(p.shape) for p in pieces],
            out_specs=whole(old.shape),
        ),
        out_shape=jax.ShapeDtypeStruct(old.shape, F32),
        compiler_params=params(),
        name="placed",
    )(jnp.stack([core, chip]), old, *pieces)


def stages(chips):
    steps, stride = [], 1
    while stride < chips:
        radix = min(RADIX, chips // stride)
        steps.append((stride, radix))
        stride *= radix
    return steps


def sum_over_chips(terms, series):
    for stride, radix in stages(series // 2):
        left = terms[0].shape[0] // radix

        def digit(k):
            return added([t.reshape((left, radix) + t.shape[1:])[:, k] for t in terms])

        got = [swap(digit(k), "series", 2 * stride * k, series) for k in range(1, radix)]
        terms = [digit(0)] + got
    return terms


def gather_over_chips(own, series):
    held = [own]
    for stride, radix in reversed(stages(series // 2)):
        if len(held) > 1:
            own = jnp.stack(held, axis=1)
            own = own.reshape((-1,) + own.shape[2:])
        held = [own] + [swap(own, "series", 2 * stride * k, series) for k in range(1, radix)]
    return held


def body(series, tm, metric, omega, psi, phi, theta, range_old, corange_old, core_old):
    me = lax.axis_index("series")
    slot = lax.axis_index("tm")
    core, chip = me % 2, me // 2
    chips = series // 2

    core_send = core_half(1 - core, chip, phi, metric, theta, chips)
    core_got = swap(core_send, "series", 1, series)
    send, far, own = range_blocks(slot, omega, metric, tm)
    range_got = swap(send, "tm", 1, tm)
    core_keep = core_half(core, chip, phi, metric, theta, chips)
    core_terms = sum_over_chips([core_keep, core_got], series)

    corange_send, corange_keep = corange_blocks(core, chip, psi, metric, chips)
    corange_got = swap(corange_send, "series", 1, series)

    core_part = added(core_terms)
    parts = [core_part] + [swap(core_part, "tm", k, tm) for k in range(1, tm)]
    while len(parts) > 1:
        parts = [a + b for a, b in zip(parts[::2], parts[1::2])]

    own = own + range_got[0]
    far = far + range_got[1:]
    distance = 2
    while distance < tm:
        near, rest = far[::2], far[1::2]
        got = swap(near, "tm", distance, tm)
        own = own + got[0]
        far = rest + got[1:]
        distance *= 2
    range_new = range_old + own.T

    corange_terms = sum_over_chips([corange_keep, corange_got], series)

    pieces = gather_over_chips(parts[0], series)
    pieces = pieces + [swap(p, "series", 1, series) for p in pieces]
    core_new = placed(core, chip, core_old, pieces, chips)
    corange_new = corange_old + added(corange_terms)[0]
    return range_new, corange_new, core_new


def solution(mesh):
    return jax.shard_map(
        functools.partial(body, mesh.shape["series"], mesh.shape["tm"]),
        mesh=mesh,
        in_specs=(
            P("series", "tm"),
            P("tm", None),
            P(None, "series"),
            P(None, "series"),
            P(None, "tm"),
            P("series", "tm"),
            P(None, ("tm", "series")),
            P(),
        ),
        out_specs=(P("series", "tm"), P(None, ("tm", "series")), P()),
        check_vma=False,
    )
```

time: 172 us -> 72.3 us (0.42)
  waiting for transfers between devices: 138 us -> 29.6 us
  starting transfers between devices: 0.13 us -> 21.2 us
  between operations: 15.5 us -> 0.83 us
  matrix products: 10.8 us -> 0 us
  Pallas kernels: 0 us -> 8.93 us
  local copies, waits for them, and re-layouts: 1.55 us -> 8.32 us
  other arithmetic: 5.84 us -> 3.12 us
    psum x1 -> x0, waiting for transfers between devices: 138 us -> none  [body(): core_sum = lax.psum(core_term, ('series', 'tm'))]
    ppermute x0 -> x20, waiting for transfers between devices: none -> 29.6 us  [swap(): return lax.ppermute(value, axis, [(i, i ^ bits) for i in range(size)])]
    ppermute x0 -> x20, starting transfers between devices: none -> 21.2 us  [swap(): return lax.ppermute(value, axis, [(i, i ^ bits) for i in range(size)])]
    dot_general x4 -> x0, matrix products: 10.8 us -> none  [the longest x1 2.86 us: body(): range_term = jnp.dot(metric, omega, preferred_element_type=jnp.float32)]
    pallas_call x0 -> x5, Pallas kernels: none -> 8.93 us  [the longest x2 3.66 us: core_half(): pl.pallas_call(functools.partial(core_kernel, parts), grid_spec=pltpu.Pre...]
    unnamed x10 -> x28, local copies, waits for them, and re-layouts: 1.55 us -> 5.78 us
    add x3 -> x7, other arithmetic: 5.84 us -> 2.97 us  [the longest x3 1.29 us: added(): return functools.reduce(operator.add, terms)]
  transfers between devices with their start and end apart: 3 -> 20, of which waited for: 1 -> 10; matrix products, arithmetic and copies ran while one was open for 6% -> 7% of each run, Pallas kernels for 0% -> 10%
where the time goes in v1:
time: 72.3 us; the launch traced here: 71.9 us
  waiting for transfers between devices  29.6 us (41%)
  starting transfers between devices  21.2 us (29%)
  Pallas kernels  8.93 us (12%)
  local copies, waits for them, and re-layouts  8.32 us (12%)
  other arithmetic  3.12 us (4%)
  between operations  0.83 us (1%)
    ppermute x20, waiting for transfers between devices, swap(): return lax.ppermute(value, axis, [(i, i ^ bits) for i in range(size)])  29.6 us
    ppermute x20, starting transfers between devices, swap(): return lax.ppermute(value, axis, [(i, i ^ bits) for i in range(size)])  21.2 us
    unnamed x28, local copies, waits for them, and re-layouts  5.78 us
    pallas_call x2, Pallas kernels, core_half(): pl.pallas_call(functools.partial(core_kernel, parts), grid_spec=pltpu.Pre...  3.66 us
    pallas_call x1, Pallas kernels, corange_blocks(): pl.pallas_call(corange_kernel, grid_spec=pltpu.PrefetchScalarGridSpec(num...  2.84 us
    pallas_call x1, Pallas kernels, placed(): pl.pallas_call(functools.partial(place_kernel, rows, parts, len(pieces) /...  1.62 us
  transfers between devices with their start and end apart: 20, of which 10 were waited for; matrix products, arithmetic and copies ran while one was open for 7% of the time, Pallas kernels for 10%

profile of v1, /device:TPU:0, one launch (start us, length us, event | category | flops | bytes accessed | tf_op | source)
XLA Modules:
  0.0 71.9 jit_solution(8258160131505274563)
XLA Ops:
  0.7 0.1 pad_add_fusion
  0.7 1.6 %copy-done = bf16[1024,1024]{1,0:T(8,128)(2,1)S(1)} copy-done((bf16[1024,1024]{1,0:T(8,128)(2,1)S(1)}, bf16[1024,1024]{1,0:T(8,128)(2,1)}, u32[]{:S(2)}) %copy-start) | copy-done | bytes 2097176
  2.3 1.2 %copy-done.2 = bf16[512,1024]{1,0:T(8,128)(2,1)S(1)} copy-done((bf16[512,1024]{1,0:T(8,128)(2,1)S(1)}, bf16[512,1024]{1,0:T(8,128)(2,1)}, u32[]{:S(2)}) %copy-start.2) | copy-done | bytes 1048600
  3.5 1.2 %copy-done.4 = bf16[512,1024]{1,0:T(8,128)(2,1)S(1)} copy-done((bf16[512,1024]{1,0:T(8,128)(2,1)S(1)}, bf16[512,1024]{1,0:T(8,128)(2,1)}, u32[]{:S(2)}) %copy-start.4) | copy-done | bytes 1048600
  4.8 1.8 %core_half.3 = f32[4,64,512]{2,1,0:T(8,128)S(1)} custom-call(s32[2]{0:T(128)S(1)} %get-tuple-element.20.at_ref, bf16[512,1024]{1,0:T(8,128)(2,1)S(1)} %copy-done.2, bf16[1024,1024]{1,0:T(8,128)(2,1)S(1)} %copy-done, bf16[512,1024]{1,0:T(8,128)(2,1)S(1)} %copy-done.4), custom_call_target="tpu_custom_call" | custom-call | tf_op jit(solution)/shard_map/core_half/pallas_call | solution.py:51
  6.6 0.5 collective-permute-start.6
  7.1 2.8 %corange_blocks.1 = (f32[4,513,128]{2,1,0:T(8,128)S(1)}, f32[4,513,128]{2,1,0:T(8,128)S(1)}) custom-call(s32[2]{0:T(128)S(1)} %get-tuple-element.19.at_ref, bf16[513,1024]{1,0:T(8,128)(2,1)S(1)} %copy-done.8, bf16[1024,1024]{1,0:T(8,128)(2,1)S(1)} %copy-done), custom_call_target="tpu_custom_call" | custom-call | tf_op jit(solution)/shard_map/corange_blocks/pallas_call | solution.py:124
  10.0 1.2 %copy.11 = f32[4,513,128]{2,0,1:T(4,128)} copy(f32[4,513,128]{2,1,0:T(8,128)S(1)} %get-tuple-element.12) | data formatting | bytes 2101248 | tf_op jit(solution)/shard_map/corange_blocks/pallas_call | solution.py:124
  11.3 0.1 collective-permute-start.2
  11.3 0.1 pad_add_fusion.1.at_ref
  11.4 0.6 copy-done.3
  12.0 0.3 copy-done.5
  12.3 1.8 %core_half.2 = f32[4,64,512]{2,1,0:T(8,128)S(1)} custom-call(s32[2]{0:T(128)S(1)} %pad_add_fusion.1.at_ref, bf16[512,1024]{1,0:T(8,128)(2,1)S(1)} %copy-done.3, bf16[1024,1024]{1,0:T(8,128)(2,1)S(1)} %copy-done, bf16[512,1024]{1,0:T(8,128)(2,1)S(1)} %copy-done.5), custom_call_target="tpu_custom_call" | custom-call | tf_op jit(solution)/shard_map/core_half/pallas_call | solution.py:51
  14.2 0.8 %copy-done.11 = f32[4,64,512]{2,1,0:T(8,128)} copy-done((f32[4,64,512]{2,1,0:T(8,128)}, f32[4,64,512]{2,1,0:T(8,128)S(1)}, u32[]{:S(2)}) %copy-start.11) | copy-done | bytes 524312
  15.0 0.1 fusion.15
  15.0 3.5 %collective-permute-start.9 = (f32[1,64,512]{2,1,0:T(8,128)S(1)}, f32[1,64,512]{2,1,0:T(8,128)}, u32[]{:S(2)}, u32[]{:S(2)}) collective-permute-start(f32[1,64,512]{2,1,0:T(8,128)S(1)} %get-tuple-element.17), channel_id=1, source_target_pairs={{0,24},{4,28},{8,16},{12,20},{16,8},{20,12},{24,0},{28,4},{1,25},{... | collective-permute-start | bytes 393224 | tf_op jit(solution)/shard_map/ppermute | solution.py:21
  18.6 0.5 collective-permute-start.8
  19.1 0.1 collective-permute-start.7
  19.2 0.8 %range_blocks.1 = (f32[2,64,1024]{2,1,0:T(8,128)S(1)}, f32[1,64,1024]{2,1,0:T(8,128)S(1)}, f32[64,1024]{1,0:T(8,128)S(1)}) custom-call(s32[1]{0:T(128)} %bitcast.at_ref, bf16[1024,256]{1,0:T(8,128)(2,1)S(1)} %copy-done.10, bf16[1024,1024]{1,0:T(8,128)(2,1)S(1)} %copy-done.1), custom_call_target="tpu_custom_call" | custom-call | tf_op jit(solution)/shard_map/range_blocks/pallas_call | solution.py:91
  20.0 2.0 %collective-permute-start = (f32[2,64,1024]{2,1,0:T(8,128)S(1)}, f32[2,64,1024]{2,1,0:T(8,128)S(1)}, u32[]{:S(2)}, u32[]{:S(2)}) collective-permute-start(f32[2,64,1024]{2,1,0:T(8,128)S(1)} %get-tuple-element.9), channel_id=1, source_target_pairs={{0,1},{1,0},{2,3},{3,2},{4,5},{5,4},{6,7},{7,6},{8,9},{9,8},{10,11... | collective-permute-start | bytes 1572872 | tf_op jit(solution)/shard_map/ppermute | solution.py:21
  22.1 0.9 %collective-permute-done.9 = f32[1,64,512]{2,1,0:T(8,128)} collective-permute-done((f32[1,64,512]{2,1,0:T(8,128)S(1)}, f32[1,64,512]{2,1,0:T(8,128)}, u32[]{:S(2)}, u32[]{:S(2)}) %collective-permute-start.9) | collective-permute-done | bytes 131104 | tf_op jit(solution)/shard_map/ppermute | solution.py:21
  22.9 2.7 %collective-permute-done.8 = f32[1,64,512]{2,1,0:T(8,128)} collective-permute-done((f32[1,64,512]{2,1,0:T(8,128)S(1)}, f32[1,64,512]{2,1,0:T(8,128)}, u32[]{:S(2)}, u32[]{:S(2)}) %collective-permute-start.8) | collective-permute-done | bytes 131104 | tf_op jit(solution)/shard_map/ppermute | solution.py:21
  25.6 0.3 collective-permute-done.7
  25.9 1.1 %fusion.19 = f32[1,64,512]{2,1,0:T(8,128)S(1)} fusion(f32[1,64,512]{2,1,0:T(8,128)} %collective-permute-done.9, f32[1,64,512]{2,1,0:T(8,128)} %collective-permute-done.8, f32[1,64,512]{2,1,0:T(8,128)} %collective-permute-done.7, f32[1,4,64,512]{3,2,1,0:T(8,128)} %bitcast.69, f32[1,4,64,512]{3,2,1,0:T(8,128)S(1)} %bitcast.63), kind=kLoop, calls=%fused_computation.30 | loop fusion | flops 131072 | bytes 786432 | tf_op jit(solution)/shard_map/add | solution.py:17
  27.1 2.7 %collective-permute-start.11 = (f32[1,64,512]{2,1,0:T(8,128)S(1)}, f32[1,64,512]{2,1,0:T(8,128)S(1)}, u32[]{:S(2)}, u32[]{:S(2)}) collective-permute-start(f32[1,64,512]{2,1,0:T(8,128)S(1)} %fusion.19), channel_id=1, source_target_pairs={{0,2},{1,3},{2,0},{3,1},{4,6},{5,7},{6,4},{7,5},{8,10},{9,11},{10,... | collective-permute-start | bytes 393224 | tf_op jit(solution)/shard_map/ppermute | solution.py:21
  29.7 1.3 %collective-permute-start.12 = (f32[1,64,512]{2,1,0:T(8,128)S(1)}, f32[1,64,512]{2,1,0:T(8,128)S(1)}, u32[]{:S(2)}, u32[]{:S(2)}) collective-permute-start(f32[1,64,512]{2,1,0:T(8,128)S(1)} %fusion.19), channel_id=1, source_target_pairs={{0,3},{1,2},{2,1},{3,0},{4,7},{5,6},{6,5},{7,4},{8,11},{9,10},{10,... | collective-permute-start | bytes 393224 | tf_op jit(solution)/shard_map/ppermute | solution.py:21
  31.1 0.2 collective-permute-start.10
  31.3 6.0 %collective-permute-done.11 = f32[1,64,512]{2,1,0:T(8,128)S(1)} collective-permute-done((f32[1,64,512]{2,1,0:T(8,128)S(1)}, f32[1,64,512]{2,1,0:T(8,128)S(1)}, u32[]{:S(2)}, u32[]{:S(2)}) %collective-permute-start.11) | collective-permute-done | bytes 131104 | tf_op jit(solution)/shard_map/ppermute | solution.py:21
  37.3 5.7 %collective-permute-done.12 = f32[1,64,512]{2,1,0:T(8,128)S(1)} collective-permute-done((f32[1,64,512]{2,1,0:T(8,128)S(1)}, f32[1,64,512]{2,1,0:T(8,128)S(1)}, u32[]{:S(2)}, u32[]{:S(2)}) %collective-permute-start.12) | collective-permute-done | bytes 131104 | tf_op jit(solution)/shard_map/ppermute | solution.py:21
  43.1 1.6 %collective-permute-start.13 = (f32[1,64,512]{2,1,0:T(8,128)S(1)}, f32[1,64,512]{2,1,0:T(8,128)S(1)}, u32[]{:S(2)}, u32[]{:S(2)}) collective-permute-start(f32[1,64,512]{2,1,0:T(8,128)S(1)} %add_add_fusion.refs_0_), channel_id=1, source_target_pairs={{0,8},{4,12},{8,0},{12,4},{16,24},{20,28},{24,16},{28,20},{1,9},{5... | collective-permute-start | bytes 393224 | tf_op jit(solution)/shard_map/ppermute | solution.py:21
  44.7 2.1 %collective-permute-start.1 = (f32[1,64,1024]{2,1,0:T(8,128)S(1)}, f32[1,64,1024]{2,1,0:T(8,128)S(1)}, u32[]{:S(2)}, u32[]{:S(2)}) collective-permute-start(f32[1,64,1024]{2,1,0:T(8,128)S(1)} %slice_add_fusion.4), channel_id=1, source_target_pairs={{0,2},{1,3},{2,0},{3,1},{4,6},{5,7},{6,4},{7,5},{8,10},{9,11},{10,... | collective-permute-start | bytes 786440 | tf_op jit(solution)/shard_map/ppermute | solution.py:21
  46.8 1.5 %collective-permute-start.14 = (f32[1,64,512]{2,1,0:T(8,128)S(1)}, f32[1,64,512]{2,1,0:T(8,128)S(1)}, u32[]{:S(2)}, u32[]{:S(2)}) collective-permute-start(f32[1,64,512]{2,1,0:T(8,128)S(1)} %add_add_fusion.refs_0_), channel_id=1, source_target_pairs={{0,16},{4,20},{8,24},{12,28},{16,0},{20,4},{24,8},{28,12},{1,17},{... | collective-permute-start | bytes 393224 | tf_op jit(solution)/shard_map/ppermute | solution.py:21
  48.2 0.5 collective-permute-start.15
  48.8 0.5 collective-permute-start.17
  49.3 1.3 %copy.14 = f32[4,513,128]{2,1,0:T(8,128)S(1)} copy(f32[4,513,128]{2,0,1:T(4,128)} %collective-permute-done.2) | data formatting | bytes 2101248 | tf_op jit(solution)/shard_map/ppermute | solution.py:21
  50.6 0.1 fusion.2
  50.7 6.6 %collective-permute-done.1 = f32[1,64,1024]{2,1,0:T(8,128)S(1)} collective-permute-done((f32[1,64,1024]{2,1,0:T(8,128)S(1)}, f32[1,64,1024]{2,1,0:T(8,128)S(1)}, u32[]{:S(2)}, u32[]{:S(2)}) %collective-permute-start.1) | collective-permute-done | bytes 262176 | tf_op jit(solution)/shard_map/ppermute | solution.py:21
  57.3 1.5 %collective-permute-start.5 = (f32[1,513,128]{2,1,0:T(8,128)S(1)}, f32[1,513,128]{2,1,0:T(8,128)S(1)}, u32[]{:S(2)}, u32[]{:S(2)}) collective-permute-start(f32[1,513,128]{2,1,0:T(8,128)S(1)} %get-tuple-element.14), channel_id=1, source_target_pairs={{0,24},{4,28},{8,16},{12,20},{16,8},{20,12},{24,0},{28,4},{1,25},{... | collective-permute-start | bytes 787976 | tf_op jit(solution)/shard_map/ppermute | solution.py:21
  58.8 0.5 collective-permute-start.4
  59.3 1.5 %collective-permute-start.3 = (f32[1,513,128]{2,1,0:T(8,128)S(1)}, f32[1,513,128]{2,1,0:T(8,128)S(1)}, u32[]{:S(2)}, u32[]{:S(2)}) collective-permute-start(f32[1,513,128]{2,1,0:T(8,128)S(1)} %get-tuple-element.13), channel_id=1, source_target_pairs={{0,8},{4,12},{8,0},{12,4},{16,24},{20,28},{24,16},{28,20},{1,9},{5... | collective-permute-start | bytes 787976 | tf_op jit(solution)/shard_map/ppermute | solution.py:21
  60.8 0.5 collective-permute-start.19
  61.3 0.8 %fusion.12 = f32[1024,64]{0,1:T(8,128)} fusion(f32[1024,64]{0,1:T(8,128)S(1)} %copy-done.13, f32[64,1024]{1,0:T(8,128)S(1)} %get-tuple-element.8, f32[2,64,1024]{2,1,0:T(8,128)S(1)} %collective-permute-done, f32[1,64,1024]{2,1,0:T(8,128)S(1)} %collective-permute-done.1), kind=kLoop, calls=%fused_computation.19 | loop fusion | flops 196608 | bytes 1310720 | tf_op jit(solution)/shard_map/add | solution.py:230
  62.1 0.1 collective-permute-done.18.refs_6_
  62.2 0.2 collective-permute-done.19.refs_7_
  62.3 1.6 %placed.1 = f32[512,512]{1,0:T(8,128)} custom-call(s32[2]{0:T(128)S(1)} %pad_add_fusion.1.at_ref, f32[512,512]{1,0:T(8,128)S(1)} %copy-done.9, f32[1,64,512]{2,1,0:T(8,128)S(1)} %add_add_fusion.refs_0_, f32[1,64,512]{2,1,0:T(8,128)S(1)} %collective-permute-done.13.refs_1_, f32[1,64,512]{2,1,0:T(8,128)S(1)} %collective-permute-done.14.refs_2_, ...), custom_call_target="tpu_custom_call" | custom-call | tf_op jit(solution)/shard_map/placed/pallas_call | solution.py:155
  64.0 3.6 %collective-permute-done.5 = f32[1,513,128]{2,1,0:T(8,128)S(1)} collective-permute-done((f32[1,513,128]{2,1,0:T(8,128)S(1)}, f32[1,513,128]{2,1,0:T(8,128)S(1)}, u32[]{:S(2)}, u32[]{:S(2)}) %collective-permute-start.5) | collective-permute-done | bytes 262688 | tf_op jit(solution)/shard_map/ppermute | solution.py:21
  67.5 3.5 %collective-permute-done.4 = f32[1,513,128]{2,1,0:T(8,128)S(1)} collective-permute-done((f32[1,513,128]{2,1,0:T(8,128)S(1)}, f32[1,513,128]{2,1,0:T(8,128)S(1)}, u32[]{:S(2)}, u32[]{:S(2)}) %collective-permute-start.4) | collective-permute-done | bytes 262688 | tf_op jit(solution)/shard_map/ppermute | solution.py:21
  71.1 0.8 %fusion.8 = f32[513,128]{1,0:T(8,128)} fusion(f32[513,128]{1,0:T(8,128)S(1)} %copy-done.12, f32[1,513,128]{2,1,0:T(8,128)S(1)} %collective-permute-done.5, f32[1,513,128]{2,1,0:T(8,128)S(1)} %collective-permute-done.4, f32[1,513,128]{2,1,0:T(8,128)S(1)} %collective-permute-done.3, f32[1,4,513,128]{3,2,1,0:T(8,128)S(1)} %bitcast.67, ...), kind=kLoop, calls=%fused_computation.13 | loop fusion | flops 328320 | bytes 1838592 | tf_op jit(solution)/shard_map/add | solution.py:237
  (36 shorter events, 0.2 us)
Async XLA Ops:
  0.7 1.6 %copy-start = (bf16[1024,1024]{1,0:T(8,128)(2,1)S(1)}, bf16[1024,1024]{1,0:T(8,128)(2,1)}, u32[]{:S(2)}) copy-start(bf16[1024,1024]{1,0:T(8,128)(2,1)} %metric_ref.7) | copy-start | bytes 6291460
  2.3 1.2 %copy-start.2 = (bf16[512,1024]{1,0:T(8,128)(2,1)S(1)}, bf16[512,1024]{1,0:T(8,128)(2,1)}, u32[]{:S(2)}) copy-start(bf16[512,1024]{1,0:T(8,128)(2,1)} %phi_ref.3) | copy-start | bytes 3145732
  3.5 1.2 %copy-start.4 = (bf16[512,1024]{1,0:T(8,128)(2,1)S(1)}, bf16[512,1024]{1,0:T(8,128)(2,1)}, u32[]{:S(2)}) copy-start(bf16[512,1024]{1,0:T(8,128)(2,1)} %theta_ref.3) | copy-start | bytes 3145732
  4.8 2.4 %copy-start.8 = (bf16[513,1024]{1,0:T(8,128)(2,1)S(1)}, bf16[513,1024]{1,0:T(8,128)(2,1)}, u32[]{:S(2)}) copy-start(bf16[513,1024]{1,0:T(8,128)(2,1)} %psi_ref.1) | copy-start | bytes 3151876
  6.6 7.6 %collective-permute-start.6 = (f32[4,64,512]{2,1,0:T(8,128)S(1)}, f32[4,64,512]{2,1,0:T(8,128)S(1)}, u32[]{:S(2)}, u32[]{:S(2)}) collective-permute-start(f32[4,64,512]{2,1,0:T(8,128)S(1)} %core_half.3), channel_id=1, source_target_pairs={{0,4},{4,0},{8,12},{12,8},{16,20},{20,16},{24,28},{28,24},{1,5},{5... | collective-permute-start | bytes 1572872 | tf_op jit(solution)/shard_map/ppermute | solution.py:21
  10.0 4.2 %copy-start.6 = (f32[4,513,128]{2,1,0:T(8,128)}, f32[4,513,128]{2,1,0:T(8,128)S(1)}, u32[]{:S(2)}) copy-start(f32[4,513,128]{2,1,0:T(8,128)S(1)} %get-tuple-element.11) | copy-start | bytes 3151876
  10.0 2.0 %copy-start.3 = (bf16[512,1024]{1,0:T(8,128)(2,1)S(1)}, bf16[512,1024]{1,0:T(8,128)(2,1)}, u32[]{:S(2)}) copy-start(bf16[512,1024]{1,0:T(8,128)(2,1)} %phi_ref.3) | copy-start | bytes 3145732
  10.0 2.3 %copy-start.5 = (bf16[512,1024]{1,0:T(8,128)(2,1)S(1)}, bf16[512,1024]{1,0:T(8,128)(2,1)}, u32[]{:S(2)}) copy-start(bf16[512,1024]{1,0:T(8,128)(2,1)} %theta_ref.3) | copy-start | bytes 3145732
  11.3 37.5 %collective-permute-start.2 = (f32[4,513,128]{2,0,1:T(4,128)}, f32[4,513,128]{2,0,1:T(4,128)}, u32[]{:S(2)}, u32[]{:S(2)}) collective-permute-start(f32[4,513,128]{2,0,1:T(4,128)} %copy.11), channel_id=1, source_target_pairs={{0,4},{4,0},{8,12},{12,8},{16,20},{20,16},{24,28},{28,24},{1,5},{5... | collective-permute-start | bytes 3151880 | tf_op jit(solution)/shard_map/ppermute | solution.py:21
  12.3 6.9 %copy-start.1 = (bf16[1024,1024]{1,0:T(8,128)(2,1)S(1)}, bf16[1024,1024]{1,0:T(8,128)(2,1)}, u32[]{:S(2)}) copy-start(bf16[1024,1024]{1,0:T(8,128)(2,1)} %metric_ref.7) | copy-start | bytes 6291460
  14.2 5.1 %copy-start.10 = (bf16[1024,256]{1,0:T(8,128)(2,1)S(1)}, bf16[1024,256]{1,0:T(8,128)(2,1)}, u32[]{:S(2)}) copy-start(bf16[1024,256]{1,0:T(8,128)(2,1)} %omega_ref.1) | copy-start | bytes 1572868
  14.2 0.8 %copy-start.11 = (f32[4,64,512]{2,1,0:T(8,128)}, f32[4,64,512]{2,1,0:T(8,128)S(1)}, u32[]{:S(2)}) copy-start(f32[4,64,512]{2,1,0:T(8,128)S(1)} %collective-permute-done.6) | copy-start | bytes 1572868
  15.0 7.9 %collective-permute-start.9 = (f32[1,64,512]{2,1,0:T(8,128)S(1)}, f32[1,64,512]{2,1,0:T(8,128)}, u32[]{:S(2)}, u32[]{:S(2)}) collective-permute-start(f32[1,64,512]{2,1,0:T(8,128)S(1)} %get-tuple-element.17), channel_id=1, source_target_pairs={{0,24},{4,28},{8,16},{12,20},{16,8},{20,12},{24,0},{28,4},{1,25},{... | collective-permute-start | bytes 393224 | tf_op jit(solution)/shard_map/ppermute | solution.py:21
  18.6 7.1 %collective-permute-start.8 = (f32[1,64,512]{2,1,0:T(8,128)S(1)}, f32[1,64,512]{2,1,0:T(8,128)}, u32[]{:S(2)}, u32[]{:S(2)}) collective-permute-start(f32[1,64,512]{2,1,0:T(8,128)S(1)} %get-tuple-element.18), channel_id=1, source_target_pairs={{0,16},{4,20},{8,24},{12,28},{16,0},{20,4},{24,8},{28,12},{1,17},{... | collective-permute-start | bytes 393224 | tf_op jit(solution)/shard_map/ppermute | solution.py:21
  19.1 6.8 %collective-permute-start.7 = (f32[1,64,512]{2,1,0:T(8,128)S(1)}, f32[1,64,512]{2,1,0:T(8,128)}, u32[]{:S(2)}, u32[]{:S(2)}) collective-permute-start(f32[1,64,512]{2,1,0:T(8,128)S(1)} %get-tuple-element.16), channel_id=1, source_target_pairs={{0,8},{4,12},{8,0},{12,4},{16,24},{20,28},{24,16},{28,20},{1,9},{5... | collective-permute-start | bytes 393224 | tf_op jit(solution)/shard_map/ppermute | solution.py:21
  20.0 24.6 %collective-permute-start = (f32[2,64,1024]{2,1,0:T(8,128)S(1)}, f32[2,64,1024]{2,1,0:T(8,128)S(1)}, u32[]{:S(2)}, u32[]{:S(2)}) collective-permute-start(f32[2,64,1024]{2,1,0:T(8,128)S(1)} %get-tuple-element.9), channel_id=1, source_target_pairs={{0,1},{1,0},{2,3},{3,2},{4,5},{5,4},{6,7},{7,6},{8,9},{9,8},{10,11... | collective-permute-start | bytes 1572872 | tf_op jit(solution)/shard_map/ppermute | solution.py:21
  27.1 10.2 %collective-permute-start.11 = (f32[1,64,512]{2,1,0:T(8,128)S(1)}, f32[1,64,512]{2,1,0:T(8,128)S(1)}, u32[]{:S(2)}, u32[]{:S(2)}) collective-permute-start(f32[1,64,512]{2,1,0:T(8,128)S(1)} %fusion.19), channel_id=1, source_target_pairs={{0,2},{1,3},{2,0},{3,1},{4,6},{5,7},{6,4},{7,5},{8,10},{9,11},{10,... | collective-permute-start | bytes 393224 | tf_op jit(solution)/shard_map/ppermute | solution.py:21
  29.7 13.3 %collective-permute-start.12 = (f32[1,64,512]{2,1,0:T(8,128)S(1)}, f32[1,64,512]{2,1,0:T(8,128)S(1)}, u32[]{:S(2)}, u32[]{:S(2)}) collective-permute-start(f32[1,64,512]{2,1,0:T(8,128)S(1)} %fusion.19), channel_id=1, source_target_pairs={{0,3},{1,2},{2,1},{3,0},{4,7},{5,6},{6,5},{7,4},{8,11},{9,10},{10,... | collective-permute-start | bytes 393224 | tf_op jit(solution)/shard_map/ppermute | solution.py:21
  31.1 12.0 %collective-permute-start.10 = (f32[1,64,512]{2,1,0:T(8,128)S(1)}, f32[1,64,512]{2,1,0:T(8,128)S(1)}, u32[]{:S(2)}, u32[]{:S(2)}) collective-permute-start(f32[1,64,512]{2,1,0:T(8,128)S(1)} %fusion.19), channel_id=1, source_target_pairs={{0,1},{1,0},{2,3},{3,2},{4,5},{5,4},{6,7},{7,6},{8,9},{9,8},{10,11... | collective-permute-start | bytes 393224 | tf_op jit(solution)/shard_map/ppermute | solution.py:21
  43.1 5.7 %collective-permute-start.13 = (f32[1,64,512]{2,1,0:T(8,128)S(1)}, f32[1,64,512]{2,1,0:T(8,128)S(1)}, u32[]{:S(2)}, u32[]{:S(2)}) collective-permute-start(f32[1,64,512]{2,1,0:T(8,128)S(1)} %add_add_fusion.refs_0_), channel_id=1, source_target_pairs={{0,8},{4,12},{8,0},{12,4},{16,24},{20,28},{24,16},{28,20},{1,9},{5... | collective-permute-start | bytes 393224 | tf_op jit(solution)/shard_map/ppermute | solution.py:21
  44.7 5.9 %copy-start.7 = (f32[4,513,128]{2,1,0:T(8,128)S(1)}, f32[4,513,128]{2,1,0:T(8,128)}, u32[]{:S(2)}) copy-start(f32[4,513,128]{2,1,0:T(8,128)} %copy-done.6) | copy-start | bytes 3151876
  44.7 12.6 %collective-permute-start.1 = (f32[1,64,1024]{2,1,0:T(8,128)S(1)}, f32[1,64,1024]{2,1,0:T(8,128)S(1)}, u32[]{:S(2)}, u32[]{:S(2)}) collective-permute-start(f32[1,64,1024]{2,1,0:T(8,128)S(1)} %slice_add_fusion.4), channel_id=1, source_target_pairs={{0,2},{1,3},{2,0},{3,1},{4,6},{5,7},{6,4},{7,5},{8,10},{9,11},{10,... | collective-permute-start | bytes 786440 | tf_op jit(solution)/shard_map/ppermute | solution.py:21
  46.8 12.1 %collective-permute-start.14 = (f32[1,64,512]{2,1,0:T(8,128)S(1)}, f32[1,64,512]{2,1,0:T(8,128)S(1)}, u32[]{:S(2)}, u32[]{:S(2)}) collective-permute-start(f32[1,64,512]{2,1,0:T(8,128)S(1)} %add_add_fusion.refs_0_), channel_id=1, source_target_pairs={{0,16},{4,20},{8,24},{12,28},{16,0},{20,4},{24,8},{28,12},{1,17},{... | collective-permute-start | bytes 393224 | tf_op jit(solution)/shard_map/ppermute | solution.py:21
  48.2 11.1 %collective-permute-start.15 = (f32[1,64,512]{2,1,0:T(8,128)S(1)}, f32[1,64,512]{2,1,0:T(8,128)S(1)}, u32[]{:S(2)}, u32[]{:S(2)}) collective-permute-start(f32[1,64,512]{2,1,0:T(8,128)S(1)} %add_add_fusion.refs_0_), channel_id=1, source_target_pairs={{0,24},{4,28},{8,16},{12,20},{16,8},{20,12},{24,0},{28,4},{1,25},{... | collective-permute-start | bytes 393224 | tf_op jit(solution)/shard_map/ppermute | solution.py:21
  48.8 12.0 %collective-permute-start.16 = (f32[1,64,512]{2,1,0:T(8,128)S(1)}, f32[1,64,512]{2,1,0:T(8,128)S(1)}, u32[]{:S(2)}, u32[]{:S(2)}) collective-permute-start(f32[1,64,512]{2,1,0:T(8,128)S(1)} %add_add_fusion.refs_0_), channel_id=1, source_target_pairs={{0,4},{4,0},{8,12},{12,8},{16,20},{20,16},{24,28},{28,24},{1,5},{5... | collective-permute-start | bytes 393224 | tf_op jit(solution)/shard_map/ppermute | solution.py:21
  48.8 12.0 %collective-permute-start.17 = (f32[1,64,512]{2,1,0:T(8,128)S(1)}, f32[1,64,512]{2,1,0:T(8,128)S(1)}, u32[]{:S(2)}, u32[]{:S(2)}) collective-permute-start(f32[1,64,512]{2,1,0:T(8,128)S(1)} %collective-permute-done.13.refs_1_), channel_id=1, source_target_pairs={{0,4},{4,0},{8,12},{12,8},{16,20},{20,16},{24,28},{28,24},{1,5},{5... | collective-permute-start | bytes 393224 | tf_op jit(solution)/shard_map/ppermute | solution.py:21
  50.6 10.7 %copy-start.13 = (f32[1024,64]{0,1:T(8,128)S(1)}, f32[1024,64]{0,1:T(8,128)}, u32[]{:S(2)}) copy-start(f32[1024,64]{0,1:T(8,128)} %param.13) | copy-start | bytes 786436
  50.7 11.7 %copy-start.9 = (f32[512,512]{1,0:T(8,128)S(1)}, f32[512,512]{1,0:T(8,128)}, u32[]{:S(2)}) copy-start(f32[512,512]{1,0:T(8,128)} %old_ref.1) | copy-start | bytes 3145732
  57.3 10.2 %collective-permute-start.5 = (f32[1,513,128]{2,1,0:T(8,128)S(1)}, f32[1,513,128]{2,1,0:T(8,128)S(1)}, u32[]{:S(2)}, u32[]{:S(2)}) collective-permute-start(f32[1,513,128]{2,1,0:T(8,128)S(1)} %get-tuple-element.14), channel_id=1, source_target_pairs={{0,24},{4,28},{8,16},{12,20},{16,8},{20,12},{24,0},{28,4},{1,25},{... | collective-permute-start | bytes 787976 | tf_op jit(solution)/shard_map/ppermute | solution.py:21
  58.8 12.3 %collective-permute-start.4 = (f32[1,513,128]{2,1,0:T(8,128)S(1)}, f32[1,513,128]{2,1,0:T(8,128)S(1)}, u32[]{:S(2)}, u32[]{:S(2)}) collective-permute-start(f32[1,513,128]{2,1,0:T(8,128)S(1)} %get-tuple-element.15), channel_id=1, source_target_pairs={{0,16},{4,20},{8,24},{12,28},{16,0},{20,4},{24,8},{28,12},{1,17},{... | collective-permute-start | bytes 787976 | tf_op jit(solution)/shard_map/ppermute | solution.py:21
  59.3 11.8 %collective-permute-start.3 = (f32[1,513,128]{2,1,0:T(8,128)S(1)}, f32[1,513,128]{2,1,0:T(8,128)S(1)}, u32[]{:S(2)}, u32[]{:S(2)}) collective-permute-start(f32[1,513,128]{2,1,0:T(8,128)S(1)} %get-tuple-element.13), channel_id=1, source_target_pairs={{0,8},{4,12},{8,0},{12,4},{16,24},{20,28},{24,16},{28,20},{1,9},{5... | collective-permute-start | bytes 787976 | tf_op jit(solution)/shard_map/ppermute | solution.py:21
  60.8 1.3 %collective-permute-start.18 = (f32[1,64,512]{2,1,0:T(8,128)S(1)}, f32[1,64,512]{2,1,0:T(8,128)S(1)}, u32[]{:S(2)}, u32[]{:S(2)}) collective-permute-start(f32[1,64,512]{2,1,0:T(8,128)S(1)} %collective-permute-done.14.refs_2_), channel_id=1, source_target_pairs={{0,4},{4,0},{8,12},{12,8},{16,20},{20,16},{24,28},{28,24},{1,5},{5... | collective-permute-start | bytes 393224 | tf_op jit(solution)/shard_map/ppermute | solution.py:21
  60.8 1.5 %collective-permute-start.19 = (f32[1,64,512]{2,1,0:T(8,128)S(1)}, f32[1,64,512]{2,1,0:T(8,128)S(1)}, u32[]{:S(2)}, u32[]{:S(2)}) collective-permute-start(f32[1,64,512]{2,1,0:T(8,128)S(1)} %collective-permute-done.15.refs_3_), channel_id=1, source_target_pairs={{0,4},{4,0},{8,12},{12,8},{16,20},{20,16},{24,28},{28,24},{1,5},{5... | collective-permute-start | bytes 393224 | tf_op jit(solution)/shard_map/ppermute | solution.py:21
  62.1 9.0 %copy-start.12 = (f32[513,128]{1,0:T(8,128)S(1)}, f32[513,128]{1,0:T(8,128)}, u32[]{:S(2)}) copy-start(f32[513,128]{1,0:T(8,128)} %param.14) | copy-start | bytes 787972

commit v2 on v1

v2 whole, which is shorter than its diff:
```python
import functools
import operator

import jax
import jax.numpy as jnp
from jax import lax
from jax.experimental import pallas as pl
from jax.experimental.pallas import tpu as pltpu
from jax.sharding import PartitionSpec as P

F32 = jnp.float32
RADIX = 4
CHUNKS = 4
DIRECT = True
VMEM_LIMIT = 8 * 1024 * 1024
BESIDE = pl.CostEstimate(flops=10**11, bytes_accessed=4 * 1024 * 1024, transcendentals=0)
FIRST_LIMIT = 60 * 1024 * 1024


def added(terms):
    return functools.reduce(operator.add, terms)


def swap(value, axis, bits, size):
    return lax.ppermute(value, axis, [(i, i ^ bits) for i in range(size)])


def params():
    return pltpu.CompilerParams(vmem_limit_bytes=VMEM_LIMIT)


def whole(shape):
    return pl.BlockSpec(shape, lambda i, at: (0,) * len(shape))


def core_kernel(
    parts, other, phi_any, metric_any, theta_any,
    out_ref, phi, metric, theta, high, low, sum_ref, sems,
):
    me = lax.axis_index("series")
    core, chip = me & 1, me >> 1
    rows, cols = phi.shape[0], metric.shape[1] // CHUNKS
    first = pl.multiple_of((core ^ other) * rows, rows)
    copies = [pltpu.make_async_copy(phi_any.at[pl.ds(first, rows), :], phi, sems.at[0])]
    for c in range(CHUNKS):
        at = slice(c * cols, (c + 1) * cols)
        copies.append(
            pltpu.make_async_copy(metric_any.at[:, at], metric.at[:, at], sems.at[1 + c])
        )
    copies.append(pltpu.make_async_copy(theta_any, theta, sems.at[1 + CHUNKS]))
    for copy in copies:
        copy.start()
    copies[0].wait()
    for c in range(CHUNKS):
        at = slice(c * cols, (c + 1) * cols)
        copies[1 + c].wait()
        left = jnp.dot(phi[...], metric[:, at], preferred_element_type=F32)
        top = left.astype(jnp.bfloat16)
        high[:, at] = top
        low[:, at] = (left - top.astype(F32)).astype(jnp.bfloat16)
    copies[-1].wait()
    by_rows = (((1,), (1,)), ((), ()))
    sum_ref[...] = lax.dot_general(high[...], theta[...], by_rows, preferred_element_type=F32)
    sum_ref[...] += lax.dot_general(low[...], theta[...], by_rows, preferred_element_type=F32)
    block = rows // parts
    for k in range(parts):
        out_ref[k] = sum_ref[pl.ds(pl.multiple_of((chip ^ k) * block, block), block), :]


def core_half(other, phi, metric, theta, parts):
    order, depth = phi.shape
    rows, cols = order // 2, theta.shape[0]
    left = (rows, metric.shape[1])
    shape = (parts, rows // parts, cols)
    return pl.pallas_call(
        functools.partial(core_kernel, parts, other),
        in_specs=[pl.BlockSpec(memory_space=pl.ANY)] * 3,
        out_specs=pl.BlockSpec(memory_space=pltpu.VMEM),
        scratch_shapes=[
            pltpu.VMEM((rows, depth), phi.dtype),
            pltpu.VMEM(metric.shape, metric.dtype),
            pltpu.VMEM(theta.shape, theta.dtype),
            pltpu.VMEM(left, jnp.bfloat16),
            pltpu.VMEM(left, jnp.bfloat16),
            pltpu.VMEM((rows, cols), F32),
            pltpu.SemaphoreType.DMA((CHUNKS + 2,)),
        ],
        out_shape=jax.ShapeDtypeStruct(shape, F32),
        compiler_params=pltpu.CompilerParams(vmem_limit_bytes=FIRST_LIMIT),
        name="core_half",
    )(phi, metric, theta)


def range_kernel(parts, at_ref, omega_ref, metric_ref, send_ref, far_ref, own_ref, sum_ref):
    slot = at_ref[0]
    sum_ref[...] = lax.dot_general(
        omega_ref[...], metric_ref[...], (((0,), (1,)), ((), ())), preferred_element_type=F32
    )
    rows = sum_ref.shape[0] // parts

    def block(k):
        return sum_ref[pl.ds(pl.multiple_of((slot ^ k) * rows, rows), rows), :]

    for j in range(parts // 2):
        send_ref[j] = block(2 * j + 1)
    for j in range(1, parts // 2):
        far_ref[j - 1] = block(2 * j)
    own_ref[...] = block(0)


def range_blocks(slot, omega, metric, parts):
    series, width = metric.shape[0], omega.shape[1]
    rows = width // parts
    shapes = [(parts // 2, rows, series), (parts // 2 - 1, rows, series), (rows, series)]
    return pl.pallas_call(
        functools.partial(range_kernel, parts),
        grid_spec=pltpu.PrefetchScalarGridSpec(
            num_scalar_prefetch=1,
            grid=(1,),
            in_specs=[whole(omega.shape), whole(metric.shape)],
            out_specs=[whole(s) for s in shapes],
            scratch_shapes=[pltpu.VMEM((width, series), F32)],
        ),
        out_shape=[jax.ShapeDtypeStruct(s, F32) for s in shapes],
        compiler_params=params(),
        name="range_blocks",
    )(jnp.stack([slot]), omega, metric)


def corange_kernel(parts, at_ref, psi_ref, metric_ref, *refs):
    chip, core = at_ref[0], at_ref[1]
    sent, kept, sum_ref = refs[:-1][: len(refs) // 2], refs[:-1][len(refs) // 2 :], refs[-1]
    rows, pair = sum_ref.shape
    cols = pair // 2
    for k in range(parts):
        first = pl.multiple_of((chip ^ k) * pair, pair)
        sum_ref[...] = jnp.dot(
            psi_ref[...], metric_ref[:, pl.ds(first, pair)], preferred_element_type=F32
        )
        for group, side in ((kept, core), (sent, 1 - core)):
            ref, j = group[k % len(group)], k // len(group)
            ref[j, :rows] = sum_ref[:, pl.ds(pl.multiple_of(side * cols, cols), cols)]
            if ref.shape[1] > rows:
                ref[j, rows:] = jnp.zeros((ref.shape[1] - rows, cols), F32)


def corange_blocks(core, chip, psi, metric, parts):
    rows, depth = psi.shape
    cols = metric.shape[1] // (2 * parts)
    radix = min(RADIX, parts)
    if cols % 128:
        term = jnp.dot(psi, metric, preferred_element_type=F32).reshape(rows, parts, 2, cols)
        term = jnp.take(term, chip ^ jnp.arange(parts), axis=1).transpose(2, 1, 0, 3)
        pick = lambda c: split(lax.dynamic_index_in_dim(term, c, 0, keepdims=False), radix)
        return pick(1 - core), pick(core)
    held = -(-rows // 8) * 8
    shape = (parts // radix, held, cols)
    blocks = pl.pallas_call(
        functools.partial(corange_kernel, parts),
        grid_spec=pltpu.PrefetchScalarGridSpec(
            num_scalar_prefetch=1,
            grid=(1,),
            in_specs=[whole(psi.shape), whole(metric.shape)],
            out_specs=[whole(shape)] * (2 * radix),
            scratch_shapes=[pltpu.VMEM((rows, 2 * cols), F32)],
        ),
        out_shape=[jax.ShapeDtypeStruct(shape, F32)] * (2 * radix),
        compiler_params=pltpu.CompilerParams(vmem_limit_bytes=2 * VMEM_LIMIT),
        cost_estimate=BESIDE,
        name="corange_blocks",
    )(jnp.stack([chip, core]), psi, metric)
    return blocks[:radix], blocks[radix:]


def range_add_kernel(own_ref, far_ref, got_ref, own_out, far_out):
    own_out[...] = own_ref[...] + got_ref[0]
    far_out[...] = far_ref[...] + got_ref[1:]


def range_add(own, far, got):
    vmem = pl.BlockSpec(memory_space=pltpu.VMEM)
    return pl.pallas_call(
        range_add_kernel,
        in_specs=[vmem] * 3,
        out_specs=[vmem] * 2,
        out_shape=[jax.ShapeDtypeStruct(a.shape, F32) for a in (own, far)],
        compiler_params=params(),
        cost_estimate=BESIDE,
        name="range_add",
    )(own, far, got)


def base_add_kernel(old_ref, own_ref, out_ref):
    out_ref[...] = old_ref[...] + own_ref[...]


def base_add(old, own):
    vmem = pl.BlockSpec(memory_space=pltpu.VMEM)
    return pl.pallas_call(
        base_add_kernel,
        in_specs=[vmem] * 2,
        out_specs=vmem,
        out_shape=jax.ShapeDtypeStruct(old.shape, F32),
        compiler_params=params(),
        cost_estimate=BESIDE,
        name="base_add",
    )(old, own)


def last_add_kernel(count, old_ref, base_ref, *refs):
    rows = old_ref.shape[0]
    corange_out, range_out = refs[-2:]
    corange_out[...] = old_ref[...] + added([r[0, :rows] for r in refs[:count]])
    range_out[...] = base_ref[...] + added([r[0] for r in refs[count:-2]])


def last_add(old, terms, base, got):
    vmem = pl.BlockSpec(memory_space=pltpu.VMEM)
    return pl.pallas_call(
        functools.partial(last_add_kernel, len(terms)),
        in_specs=[vmem] * (2 + len(terms) + len(got)),
        out_specs=[vmem] * 2,
        out_shape=[jax.ShapeDtypeStruct(a.shape, F32) for a in (old, base)],
        compiler_params=params(),
        cost_estimate=BESIDE,
        name="last_add",
    )(old, base, *terms, *got)


def place_kernel(rows, half, radix, at_ref, old_ref, *refs):
    core, chip = at_ref[0], at_ref[1]
    pieces, out_ref = refs[:-1], refs[-1]
    for i, ref in enumerate(pieces):
        side, digit = i // radix, i % radix
        for g in range(ref.shape[0]):
            row = ((core ^ side) * half + (chip ^ (g * radix + digit))) * rows
            at = pl.ds(pl.multiple_of(row, rows), rows)
            out_ref[at, :] = old_ref[at, :] + ref[g]


def placed(core, chip, old, pieces, parts):
    rows = old.shape[0] // (2 * parts)
    return pl.pallas_call(
        functools.partial(place_kernel, rows, parts, len(pieces) // 2),
        grid_spec=pltpu.PrefetchScalarGridSpec(
            num_scalar_prefetch=1,
            grid=(1,),
            in_specs=[whole(old.shape)] + [whole(p.shape) for p in pieces],
            out_specs=whole(old.shape),
        ),
        out_shape=jax.ShapeDtypeStruct(old.shape, F32),
        compiler_params=params(),
        name="placed",
    )(jnp.stack([core, chip]), old, *pieces)


def stages(chips):
    steps, stride = [], 1
    while stride < chips:
        radix = min(RADIX, chips // stride)
        steps.append((stride, radix))
        stride *= radix
    return steps


def split(value, radix):
    left = value.shape[0] // radix
    value = value.reshape((left, radix) + value.shape[1:])
    return [value[:, k] for k in range(radix)]


def sum_over_chips(terms, series):
    for stride, radix in stages(series // 2):
        if stride > 1:
            terms = [split(t, radix) for t in terms]
        sums = [added(blocks) for blocks in zip(*terms)]
        terms = sums[:1] + [swap(sums[k], "series", 2 * stride * k, series) for k in range(1, radix)]
    return terms


def gather_over_chips(own, series):
    held = [own]
    for stride, radix in reversed(stages(series // 2)):
        if len(held) > 1:
            own = jnp.stack(held, axis=1)
            own = own.reshape((-1,) + own.shape[2:])
        held = [own] + [swap(own, "series", 2 * stride * k, series) for k in range(1, radix)]
    return held


def after(value, *others):
    return lax.optimization_barrier((value,) + others)[0]


def body(series, tm, metric, omega, psi, phi, theta, range_old, corange_old, core_old):
    me = lax.axis_index("series")
    slot = lax.axis_index("tm")
    core, chip = me & 1, me >> 1
    chips = series // 2

    core_send = core_half(1, phi, metric, theta, chips)
    core_got = swap(core_send, "series", 1, series)
    core_keep = core_half(0, after(phi, core_send), metric, theta, chips)
    radix = min(RADIX, chips)
    core_terms = sum_over_chips([split(core_keep, radix), split(core_got, radix)], series)

    near, far, own = range_blocks(slot, after(omega, core_terms[0]), metric, tm)
    range_got = swap(near, "tm", 1, tm)
    corange_send, corange_keep = corange_blocks(core, chip, after(psi, near), metric, chips)
    corange_got = [swap(b, "series", 1, series) for b in corange_send]
    corange_terms = sum_over_chips([corange_keep, corange_got], series)

    core_part = added([after(t, *corange_send) for t in core_terms])
    parts = [core_part] + [swap(core_part, "tm", k, tm) for k in range(1, tm)]

    own, far = range_add(own, after(far, core_part, corange_terms[0]), range_got)
    late = []
    distance = 2
    while distance < tm:
        got = swap(far[::2], "tm", distance, tm)
        late.append(got[:1])
        far = far[1::2] + got[1:]
        distance *= 2
    base = base_add(range_old.T, own)

    parts = [after(p, base) for p in parts]
    while len(parts) > 1:
        parts = [a + b for a, b in zip(parts[::2], parts[1::2])]
    core_all = parts[0]

    corange_new, range_new = last_add(after(corange_old, core_all), corange_terms, base, late)
    pieces = gather_over_chips(core_all, series)
    pieces = pieces[:1] + [after(p, corange_new) for p in pieces[1:]]
    pieces = pieces + [swap(p, "series", 1, series) for p in pieces]
    core_new = placed(core, chip, core_old, pieces, chips)
    return range_new.T, corange_new, core_new


def solution(mesh):
    return jax.shard_map(
        functools.partial(body, mesh.shape["series"], mesh.shape["tm"]),
        mesh=mesh,
        in_specs=(
            P("series", "tm"),
            P("tm", None),
            P(None, "series"),
            P(None, "series"),
            P(None, "tm"),
            P("series", "tm"),
            P(None, ("tm", "series")),
            P(),
        ),
        out_specs=(P("series", "tm"), P(None, ("tm", "series")), P()),
        check_vma=False,
    )
```

time: 72.3 us -> 59.9 us (0.83)
  waiting for transfers between devices: 29.6 us -> 11.2 us
  local copies, waits for them, and re-layouts: 8.32 us -> 0.02 us
  Pallas kernels: 8.93 us -> 15.7 us
  starting transfers between devices: 21.2 us -> 27.3 us
  other arithmetic: 3.12 us -> 4.65 us
    ppermute x20 -> x23, waiting for transfers between devices: 29.6 us -> 11.2 us  [swap(): return lax.ppermute(value, axis, [(i, i ^ bits) for i in range(size)])]
    pallas_call x3 -> x6, Pallas kernels: 6.5 us -> 13.3 us  [the longest x2 9.22 us: core_half(): pl.pallas_call(functools.partial(core_kernel, parts, other), in_specs=[pl...]
    ppermute x20 -> x23, starting transfers between devices: 21.2 us -> 27.3 us  [swap(): return lax.ppermute(value, axis, [(i, i ^ bits) for i in range(size)])]
    unnamed x28 -> x12, local copies, waits for them, and re-layouts: 5.78 us -> 0.02 us
    add x3 -> x6, other arithmetic: 1.29 us -> 3.49 us  [added(): return functools.reduce(operator.add, terms)]
    add x3 -> x0, other arithmetic: 1.65 us -> none  [the longest x1 0.83 us: body(): corange_new = corange_old + added(corange_terms)[0]]
    ppermute x1 -> x0, local copies, waits for them, and re-layouts: 1.29 us -> none  [swap(): return lax.ppermute(value, axis, [(i, i ^ bits) for i in range(size)])]
    pallas_call x1 -> x0, local copies, waits for them, and re-layouts: 1.25 us -> none  [corange_blocks(): pl.pallas_call(corange_kernel, grid_spec=pltpu.PrefetchScalarGridSpec(num...]
  transfers between devices with their start and end apart: 20 -> 23, of which waited for: 10 -> 9; matrix products, arithmetic and copies ran while one was open for 7% -> 6% of each run, Pallas kernels for 10% -> 15%
where the time goes in v2:
time: 59.9 us; the launch traced here: 59.7 us
  starting transfers between devices  27.3 us (46%)
  Pallas kernels  15.7 us (26%)
  waiting for transfers between devices  11.2 us (19%)
  other arithmetic  4.65 us (8%)
  between operations  0.77 us (1%)
    ppermute x23, starting transfers between devices, swap(): return lax.ppermute(value, axis, [(i, i ^ bits) for i in range(size)])  27.3 us
    ppermute x23, waiting for transfers between devices, swap(): return lax.ppermute(value, axis, [(i, i ^ bits) for i in range(size)])  11.2 us
    pallas_call x2, Pallas kernels, core_half(): pl.pallas_call(functools.partial(core_kernel, parts, other), in_specs=[pl...  9.22 us
    add x6, other arithmetic, added(): return functools.reduce(operator.add, terms)  3.49 us
    pallas_call x1, Pallas kernels, corange_blocks(): pl.pallas_call(functools.partial(corange_kernel, parts), grid_spec=pltpu....  2.03 us
    pallas_call x1, Pallas kernels, last_add(): pl.pallas_call(functools.partial(last_add_kernel, len(terms)), in_specs=[...  1.93 us
    pallas_call x1, Pallas kernels, placed(): pl.pallas_call(functools.partial(place_kernel, rows, parts, len(pieces) /...  1.62 us
  transfers between devices with their start and end apart: 23, of which 9 were waited for; matrix products, arithmetic and copies ran while one was open for 6% of the time, Pallas kernels for 15%

profile of v2, /device:TPU:0, one launch (start us, length us, event | category | flops | bytes accessed | tf_op | source)
XLA Modules:
  0.0 59.7 jit_solution(4787298272145925820)
XLA Ops:
  0.6 4.5 %core_half.2 = f32[4,64,512]{2,1,0:T(8,128)} custom-call(bf16[512,1024]{1,0:T(8,128)(2,1)} %phi_any.2, bf16[1024,1024]{1,0:T(8,128)(2,1)} %metric_ref.3, bf16[512,1024]{1,0:T(8,128)(2,1)} %theta_any.3), custom_call_target="tpu_custom_call" | custom-call | tf_op jit(solution)/shard_map/core_half/pallas_call | solution.py:75
  5.2 0.5 collective-permute-start
  5.7 4.7 %core_half.3 = f32[4,64,512]{2,1,0:T(8,128)} custom-call(bf16[512,1024]{1,0:T(8,128)(2,1)} %phi_any.2, bf16[1024,1024]{1,0:T(8,128)(2,1)} %metric_ref.3, bf16[512,1024]{1,0:T(8,128)(2,1)} %theta_any.3), custom_call_target="tpu_custom_call" | custom-call | tf_op jit(solution)/shard_map/core_half/pallas_call | solution.py:75
  10.4 0.1 pad_add_fusion.at_ref
  10.5 0.0 collective-permute-done
  10.5 1.3 %fusion.2 = (f32[1,64,512]{2,1,0:T(8,128)S(1)}, f32[1,64,512]{2,1,0:T(8,128)S(1)}, f32[1,64,512]{2,1,0:T(8,128)S(1)}, f32[1,64,512]{2,1,0:T(8,128)S(1)}) fusion(f32[1,4,64,512]{3,2,1,0:T(8,128)S(1)} %bitcast.17, f32[1,4,64,512]{3,2,1,0:T(8,128)} %bitcast.16), kind=kLoop, calls=%fused_computation.5 | loop fusion | flops 131072 | bytes 1572864 | tf_op jit(solution)/shard_map/add | solution.py:21
  11.8 0.8 %range_blocks.1 = (f32[2,64,1024]{2,1,0:T(8,128)S(1)}, f32[1,64,1024]{2,1,0:T(8,128)S(1)}, f32[64,1024]{1,0:T(8,128)S(1)}) custom-call(s32[1]{0:T(128)} %bitcast.5.at_ref, bf16[1024,256]{1,0:T(8,128)(2,1)S(1)} %copy-done.2, bf16[1024,1024]{1,0:T(8,128)(2,1)S(1)} %copy-done), custom_call_target="tpu_custom_call" | custom-call | tf_op jit(solution)/shard_map/range_blocks/pallas_call | solution.py:115
  12.6 2.7 %collective-permute-start.5 = (f32[2,64,1024]{2,1,0:T(8,128)S(1)}, f32[2,64,1024]{2,1,0:T(8,128)S(1)}, u32[]{:S(2)}, u32[]{:S(2)}) collective-permute-start(f32[2,64,1024]{2,1,0:T(8,128)S(1)} %get-tuple-element.36), channel_id=1, source_target_pairs={{0,1},{1,0},{2,3},{3,2},{4,5},{5,4},{6,7},{7,6},{8,9},{9,8},{10,11... | collective-permute-start | bytes 1572872 | tf_op jit(solution)/shard_map/ppermute | solution.py:25
  15.3 1.5 %collective-permute-start.1 = (f32[1,64,512]{2,1,0:T(8,128)S(1)}, f32[1,64,512]{2,1,0:T(8,128)S(1)}, u32[]{:S(2)}, u32[]{:S(2)}) collective-permute-start(f32[1,64,512]{2,1,0:T(8,128)S(1)} %get-tuple-element.65), channel_id=1, source_target_pairs={{0,8},{4,12},{8,0},{12,4},{16,24},{20,28},{24,16},{28,20},{1,9},{5... | collective-permute-start | bytes 393224 | tf_op jit(solution)/shard_map/ppermute | solution.py:25
  16.8 1.5 %collective-permute-start.2 = (f32[1,64,512]{2,1,0:T(8,128)S(1)}, f32[1,64,512]{2,1,0:T(8,128)S(1)}, u32[]{:S(2)}, u32[]{:S(2)}) collective-permute-start(f32[1,64,512]{2,1,0:T(8,128)S(1)} %get-tuple-element.67), channel_id=1, source_target_pairs={{0,16},{4,20},{8,24},{12,28},{16,0},{20,4},{24,8},{28,12},{1,17},{... | collective-permute-start | bytes 393224 | tf_op jit(solution)/shard_map/ppermute | solution.py:25
  18.3 0.5 collective-permute-start.3
  18.8 2.0 %corange_blocks.1 = (f32[1,520,128]{2,1,0:T(8,128)S(1)}, f32[1,520,128]{2,1,0:T(8,128)S(1)}, f32[1,520,128]{2,1,0:T(8,128)S(1)}, f32[1,520,128]{2,1,0:T(8,128)S(...) custom-call(s32[2]{0:T(128)S(1)} %pad_add_fusion.at_ref, ...), custom_call_target="tpu_custom_call" | custom-call | flops 99999997952 | bytes 4194304 | tf_op jit(solution)/shard_map/corange_blocks/pallas_call | solution.py:158
  20.8 0.1 collective-permute-start.4
  20.9 0.3 collective-permute-done.1
  21.2 0.2 collective-permute-start.13
  21.4 3.5 %collective-permute-done.2 = f32[1,64,512]{2,1,0:T(8,128)S(1)} collective-permute-done((f32[1,64,512]{2,1,0:T(8,128)S(1)}, f32[1,64,512]{2,1,0:T(8,128)S(1)}, u32[]{:S(2)}, u32[]{:S(2)}) %collective-permute-start.2) | collective-permute-done | bytes 131104 | tf_op jit(solution)/shard_map/ppermute | solution.py:25
  24.9 0.5 collective-permute-start.9
  25.4 0.7 %add_add_fusion.1 = f32[1,64,512]{2,1,0:T(8,128)} fusion(f32[1,64,512]{2,1,0:T(8,128)S(1)} %collective-permute-done.3, f32[1,64,512]{2,1,0:T(8,128)S(1)} %collective-permute-done.2, f32[1,64,512]{2,1,0:T(8,128)S(1)} %get-tuple-element.42, f32[1,64,512]{2,1,0:T(8,128)S(1)} %collective-permute-done.1), kind=kLoop, calls=%fused_computation.9 | loop fusion | flops 98304 | bytes 655360 | tf_op jit(solution)/shard_map/add | solution.py:21
  26.1 0.4 collective-permute-start.6
  26.6 3.7 %collective-permute-start.8 = (f32[1,64,512]{2,1,0:T(8,128)}, f32[1,64,512]{2,1,0:T(8,128)S(1)}, u32[]{:S(2)}, u32[]{:S(2)}) collective-permute-start(f32[1,64,512]{2,1,0:T(8,128)} %add_add_fusion.1), channel_id=1, source_target_pairs={{0,3},{1,2},{2,1},{3,0},{4,7},{5,6},{6,5},{7,4},{8,11},{9,10},{10,... | collective-permute-start | bytes 393224 | tf_op jit(solution)/shard_map/ppermute | solution.py:25
  30.2 0.7 %add.103 = f32[1,520,128]{2,1,0:T(8,128)} add(f32[1,520,128]{2,1,0:T(8,128)S(1)} %get-tuple-element.58, f32[1,520,128]{2,1,0:T(8,128)S(1)} %collective-permute-done.13) | non-fusion elementwise | flops 66560 | bytes 798720 | tf_op jit(solution)/shard_map/add | solution.py:21
  31.0 0.0 collective-permute-done.11
  31.0 0.7 %add.102 = f32[1,520,128]{2,1,0:T(8,128)} add(f32[1,520,128]{2,1,0:T(8,128)S(1)} %get-tuple-element.57, f32[1,520,128]{2,1,0:T(8,128)S(1)} %collective-permute-done.11) | non-fusion elementwise | flops 66560 | bytes 798720 | tf_op jit(solution)/shard_map/add | solution.py:21
  31.7 0.0 collective-permute-done.9
  31.7 1.5 %collective-permute-start.14 = (f32[1,520,128]{2,1,0:T(8,128)}, f32[1,520,128]{2,1,0:T(8,128)}, u32[]{:S(2)}, u32[]{:S(2)}) collective-permute-start(f32[1,520,128]{2,1,0:T(8,128)} %add.103), channel_id=1, source_target_pairs={{0,24},{4,28},{8,16},{12,20},{16,8},{20,12},{24,0},{28,4},{1,25},{... | collective-permute-start | bytes 798728 | tf_op jit(solution)/shard_map/ppermute | solution.py:25
  33.2 0.0 collective-permute-done.5.got_ref
  33.3 0.8 %collective-permute-start.12 = (f32[1,520,128]{2,1,0:T(8,128)}, f32[1,520,128]{2,1,0:T(8,128)}, u32[]{:S(2)}, u32[]{:S(2)}) collective-permute-start(f32[1,520,128]{2,1,0:T(8,128)} %add.102), channel_id=1, source_target_pairs={{0,16},{4,20},{8,24},{12,28},{16,0},{20,4},{24,8},{28,12},{1,17},{... | collective-permute-start | bytes 798728 | tf_op jit(solution)/shard_map/ppermute | solution.py:25
  34.0 0.1 range_add.1
  34.1 1.4 %collective-permute-start.10 = (f32[1,520,128]{2,1,0:T(8,128)S(1)}, f32[1,520,128]{2,1,0:T(8,128)S(1)}, u32[]{:S(2)}, u32[]{:S(2)}) collective-permute-start(f32[1,520,128]{2,1,0:T(8,128)S(1)} %add.101), channel_id=1, source_target_pairs={{0,8},{4,12},{8,0},{12,4},{16,24},{20,28},{24,16},{28,20},{1,9},{5... | collective-permute-start | bytes 798728 | tf_op jit(solution)/shard_map/ppermute | solution.py:25
  35.5 2.1 %collective-permute-done.8 = f32[1,64,512]{2,1,0:T(8,128)S(1)} collective-permute-done((f32[1,64,512]{2,1,0:T(8,128)}, f32[1,64,512]{2,1,0:T(8,128)S(1)}, u32[]{:S(2)}, u32[]{:S(2)}) %collective-permute-start.8) | collective-permute-done | bytes 131104 | tf_op jit(solution)/shard_map/ppermute | solution.py:25
  37.6 6.5 %collective-permute-start.15 = (f32[1,64,1024]{2,1,0:T(8,128)S(1)}, f32[1,64,1024]{2,1,0:T(8,128)S(1)}, u32[]{:S(2)}, u32[]{:S(2)}) collective-permute-start(f32[1,64,1024]{2,1,0:T(8,128)S(1)} %get-tuple-element.59), channel_id=1, source_target_pairs={{0,2},{1,3},{2,0},{3,1},{4,6},{5,7},{6,4},{7,5},{8,10},{9,11},{10,... | collective-permute-start | bytes 786440 | tf_op jit(solution)/shard_map/ppermute | solution.py:25
  44.1 1.1 %collective-permute-done.7 = f32[1,64,512]{2,1,0:T(8,128)} collective-permute-done((f32[1,64,512]{2,1,0:T(8,128)}, f32[1,64,512]{2,1,0:T(8,128)}, u32[]{:S(2)}, u32[]{:S(2)}) %collective-permute-start.7) | collective-permute-done | bytes 131104 | tf_op jit(solution)/shard_map/ppermute | solution.py:25
  45.2 1.0 %add_add_fusion.refs_0_ = f32[1,64,512]{2,1,0:T(8,128)S(1)} fusion(f32[1,64,512]{2,1,0:T(8,128)} %collective-permute-done.7, f32[1,64,512]{2,1,0:T(8,128)S(1)} %collective-permute-done.8, f32[1,64,512]{2,1,0:T(8,128)} %add_add_fusion.1, f32[1,64,512]{2,1,0:T(8,128)S(1)} %collective-permute-done.6), kind=kLoop, calls=%fused_computation.8 | loop fusion | flops 98304 | bytes 655360 | tf_op jit(solution)/shard_map/add | solution.py:328
  46.2 0.0 copy-start.1
  46.2 1.6 %collective-permute-start.18 = (f32[1,64,512]{2,1,0:T(8,128)S(1)}, f32[1,64,512]{2,1,0:T(8,128)S(1)}, u32[]{:S(2)}, u32[]{:S(2)}) collective-permute-start(f32[1,64,512]{2,1,0:T(8,128)S(1)} %add_add_fusion.refs_0_), channel_id=1, source_target_pairs={{0,24},{4,28},{8,16},{12,20},{16,8},{20,12},{24,0},{28,4},{1,25},{... | collective-permute-start | bytes 393224 | tf_op jit(solution)/shard_map/ppermute | solution.py:25
  47.9 3.9 %collective-permute-start.17 = (f32[1,64,512]{2,1,0:T(8,128)S(1)}, f32[1,64,512]{2,1,0:T(8,128)S(1)}, u32[]{:S(2)}, u32[]{:S(2)}) collective-permute-start(f32[1,64,512]{2,1,0:T(8,128)S(1)} %add_add_fusion.refs_0_), channel_id=1, source_target_pairs={{0,16},{4,20},{8,24},{12,28},{16,0},{20,4},{24,8},{28,12},{1,17},{... | collective-permute-start | bytes 393224 | tf_op jit(solution)/shard_map/ppermute | solution.py:25
  51.7 0.0 collective-permute-done.12.refs_2_
  51.7 0.0 collective-permute-start.16
  51.8 0.1 collective-permute-start.19
  51.8 1.3 %collective-permute-done.15.refs_4_ = f32[1,64,1024]{2,1,0:T(8,128)S(1)} collective-permute-done((f32[1,64,1024]{2,1,0:T(8,128)S(1)}, f32[1,64,1024]{2,1,0:T(8,128)S(1)}, u32[]{:S(2)}, u32[]{:S(2)}) %collective-permute-start.15) | collective-permute-done | bytes 262176 | tf_op jit(solution)/shard_map/ppermute | solution.py:25
  53.1 1.9 %last_add.1 = (f32[513,128]{1,0:T(8,128)}, f32[64,1024]{1,0:T(8,128)}) custom-call(f32[513,128]{1,0:T(8,128)S(1)} %copy-done.4, f32[64,1024]{1,0:T(8,128)S(1)} %base_add.1.base_ref, f32[1,520,128]{2,1,0:T(8,128)S(1)} %add.97.refs_0_, f32[1,520,128]{2,1,0:T(8,128)S(1)} %collective-permute-done.10.refs_1_, f32[1,520,128]{2,1,0:T(8,128)} %collective-permute-done.12.refs_2_, ...), custom_call_target="tpu_custom_call" | custom-call | flops 99999997952 | bytes 4194304 | tf_op jit(solution)/shard_map/last_add/pallas_call | solution.py:219
  55.0 0.6 %collective-permute-done.17.refs_2_ = f32[1,64,512]{2,1,0:T(8,128)S(1)} collective-permute-done((f32[1,64,512]{2,1,0:T(8,128)S(1)}, f32[1,64,512]{2,1,0:T(8,128)S(1)}, u32[]{:S(2)}, u32[]{:S(2)}) %collective-permute-start.17) | collective-permute-done | bytes 131104 | tf_op jit(solution)/shard_map/ppermute | solution.py:25
  55.7 0.0 collective-permute-start.21
  55.7 1.0 %collective-permute-done.16.refs_1_ = f32[1,64,512]{2,1,0:T(8,128)S(1)} collective-permute-done((f32[1,64,512]{2,1,0:T(8,128)S(1)}, f32[1,64,512]{2,1,0:T(8,128)S(1)}, u32[]{:S(2)}, u32[]{:S(2)}) %collective-permute-start.16) | collective-permute-done | bytes 131104 | tf_op jit(solution)/shard_map/ppermute | solution.py:25
  56.7 0.1 pad_add_fusion.1.at_ref
  56.8 0.2 collective-permute-done.21.refs_6_
  57.0 1.1 %collective-permute-done.20.refs_5_ = f32[1,64,512]{2,1,0:T(8,128)S(1)} collective-permute-done((f32[1,64,512]{2,1,0:T(8,128)S(1)}, f32[1,64,512]{2,1,0:T(8,128)S(1)}, u32[]{:S(2)}, u32[]{:S(2)}) %collective-permute-start.20) | collective-permute-done | bytes 131104 | tf_op jit(solution)/shard_map/ppermute | solution.py:25
  58.1 1.6 %placed.1 = f32[512,512]{1,0:T(8,128)} custom-call(s32[2]{0:T(128)S(1)} %pad_add_fusion.1.at_ref, f32[512,512]{1,0:T(8,128)S(1)} %copy-done.1, f32[1,64,512]{2,1,0:T(8,128)S(1)} %add_add_fusion.refs_0_, f32[1,64,512]{2,1,0:T(8,128)S(1)} %collective-permute-done.16.refs_1_, f32[1,64,512]{2,1,0:T(8,128)S(1)} %collective-permute-done.17.refs_2_, ...), custom_call_target="tpu_custom_call" | custom-call | tf_op jit(solution)/shard_map/placed/pallas_call | solution.py:243
  (27 shorter events, 0.2 us)
Async XLA Ops:
  5.2 5.3 %collective-permute-start = (f32[4,64,512]{2,1,0:T(8,128)}, f32[4,64,512]{2,1,0:T(8,128)S(1)}, u32[]{:S(2)}, u32[]{:S(2)}) collective-permute-start(f32[4,64,512]{2,1,0:T(8,128)} %core_half.2), channel_id=1, source_target_pairs={{0,4},{4,0},{8,12},{12,8},{16,20},{20,16},{24,28},{28,24},{1,5},{5... | collective-permute-start | bytes 1572872 | tf_op jit(solution)/shard_map/ppermute | solution.py:25
  5.7 6.0 %copy-start = (bf16[1024,1024]{1,0:T(8,128)(2,1)S(1)}, bf16[1024,1024]{1,0:T(8,128)(2,1)}, u32[]{:S(2)}) copy-start(bf16[1024,1024]{1,0:T(8,128)(2,1)} %metric_ref.3) | copy-start | bytes 6291460
  5.7 6.0 %copy-start.2 = (bf16[1024,256]{1,0:T(8,128)(2,1)S(1)}, bf16[1024,256]{1,0:T(8,128)(2,1)}, u32[]{:S(2)}) copy-start(bf16[1024,256]{1,0:T(8,128)(2,1)} %omega_ref) | copy-start | bytes 1572868
  10.5 8.3 %copy-start.3 = (bf16[513,1024]{1,0:T(8,128)(2,1)S(1)}, bf16[513,1024]{1,0:T(8,128)(2,1)}, u32[]{:S(2)}) copy-start(bf16[513,1024]{1,0:T(8,128)(2,1)} %psi_ref) | copy-start | bytes 3151876
  12.6 20.7 %collective-permute-start.5 = (f32[2,64,1024]{2,1,0:T(8,128)S(1)}, f32[2,64,1024]{2,1,0:T(8,128)S(1)}, u32[]{:S(2)}, u32[]{:S(2)}) collective-permute-start(f32[2,64,1024]{2,1,0:T(8,128)S(1)} %get-tuple-element.36), channel_id=1, source_target_pairs={{0,1},{1,0},{2,3},{3,2},{4,5},{5,4},{6,7},{7,6},{8,9},{9,8},{10,11... | collective-permute-start | bytes 1572872 | tf_op jit(solution)/shard_map/ppermute | solution.py:25
  15.3 5.9 %collective-permute-start.1 = (f32[1,64,512]{2,1,0:T(8,128)S(1)}, f32[1,64,512]{2,1,0:T(8,128)S(1)}, u32[]{:S(2)}, u32[]{:S(2)}) collective-permute-start(f32[1,64,512]{2,1,0:T(8,128)S(1)} %get-tuple-element.65), channel_id=1, source_target_pairs={{0,8},{4,12},{8,0},{12,4},{16,24},{20,28},{24,16},{28,20},{1,9},{5... | collective-permute-start | bytes 393224 | tf_op jit(solution)/shard_map/ppermute | solution.py:25
  16.8 8.1 %collective-permute-start.2 = (f32[1,64,512]{2,1,0:T(8,128)S(1)}, f32[1,64,512]{2,1,0:T(8,128)S(1)}, u32[]{:S(2)}, u32[]{:S(2)}) collective-permute-start(f32[1,64,512]{2,1,0:T(8,128)S(1)} %get-tuple-element.67), channel_id=1, source_target_pairs={{0,16},{4,20},{8,24},{12,28},{16,0},{20,4},{24,8},{28,12},{1,17},{... | collective-permute-start | bytes 393224 | tf_op jit(solution)/shard_map/ppermute | solution.py:25
  18.3 6.6 %collective-permute-start.3 = (f32[1,64,512]{2,1,0:T(8,128)S(1)}, f32[1,64,512]{2,1,0:T(8,128)S(1)}, u32[]{:S(2)}, u32[]{:S(2)}) collective-permute-start(f32[1,64,512]{2,1,0:T(8,128)S(1)} %get-tuple-element.66), channel_id=1, source_target_pairs={{0,24},{4,28},{8,16},{12,20},{16,8},{20,12},{24,0},{28,4},{1,25},{... | collective-permute-start | bytes 393224 | tf_op jit(solution)/shard_map/ppermute | solution.py:25
  20.8 5.3 %collective-permute-start.4 = (f32[1,520,128]{2,1,0:T(8,128)S(1)}, f32[1,520,128]{2,1,0:T(8,128)S(1)}, u32[]{:S(2)}, u32[]{:S(2)}) collective-permute-start(f32[1,520,128]{2,1,0:T(8,128)S(1)} %get-tuple-element.38), channel_id=1, source_target_pairs={{0,4},{4,0},{8,12},{12,8},{16,20},{20,16},{24,28},{28,24},{1,5},{5... | collective-permute-start | bytes 798728 | tf_op jit(solution)/shard_map/ppermute | solution.py:25
  21.2 5.4 %collective-permute-start.13 = (f32[1,520,128]{2,1,0:T(8,128)S(1)}, f32[1,520,128]{2,1,0:T(8,128)S(1)}, u32[]{:S(2)}, u32[]{:S(2)}) collective-permute-start(f32[1,520,128]{2,1,0:T(8,128)S(1)} %get-tuple-element.41), channel_id=1, source_target_pairs={{0,4},{4,0},{8,12},{12,8},{16,20},{20,16},{24,28},{28,24},{1,5},{5... | collective-permute-start | bytes 798728 | tf_op jit(solution)/shard_map/ppermute | solution.py:25
  24.9 6.1 %collective-permute-start.11 = (f32[1,520,128]{2,1,0:T(8,128)S(1)}, f32[1,520,128]{2,1,0:T(8,128)S(1)}, u32[]{:S(2)}, u32[]{:S(2)}) collective-permute-start(f32[1,520,128]{2,1,0:T(8,128)S(1)} %get-tuple-element.40), channel_id=1, source_target_pairs={{0,4},{4,0},{8,12},{12,8},{16,20},{20,16},{24,28},{28,24},{1,5},{5... | collective-permute-start | bytes 798728 | tf_op jit(solution)/shard_map/ppermute | solution.py:25
  24.9 6.8 %collective-permute-start.9 = (f32[1,520,128]{2,1,0:T(8,128)S(1)}, f32[1,520,128]{2,1,0:T(8,128)S(1)}, u32[]{:S(2)}, u32[]{:S(2)}) collective-permute-start(f32[1,520,128]{2,1,0:T(8,128)S(1)} %get-tuple-element.39), channel_id=1, source_target_pairs={{0,4},{4,0},{8,12},{12,8},{16,20},{20,16},{24,28},{28,24},{1,5},{5... | collective-permute-start | bytes 798728 | tf_op jit(solution)/shard_map/ppermute | solution.py:25
  26.1 8.0 %collective-permute-start.6 = (f32[1,64,512]{2,1,0:T(8,128)}, f32[1,64,512]{2,1,0:T(8,128)S(1)}, u32[]{:S(2)}, u32[]{:S(2)}) collective-permute-start(f32[1,64,512]{2,1,0:T(8,128)} %add_add_fusion.1), channel_id=1, source_target_pairs={{0,1},{1,0},{2,3},{3,2},{4,5},{5,4},{6,7},{7,6},{8,9},{9,8},{10,11... | collective-permute-start | bytes 393224 | tf_op jit(solution)/shard_map/ppermute | solution.py:25
  26.6 11.0 %collective-permute-start.8 = (f32[1,64,512]{2,1,0:T(8,128)}, f32[1,64,512]{2,1,0:T(8,128)S(1)}, u32[]{:S(2)}, u32[]{:S(2)}) collective-permute-start(f32[1,64,512]{2,1,0:T(8,128)} %add_add_fusion.1), channel_id=1, source_target_pairs={{0,3},{1,2},{2,1},{3,0},{4,7},{5,6},{6,5},{7,4},{8,11},{9,10},{10,... | collective-permute-start | bytes 393224 | tf_op jit(solution)/shard_map/ppermute | solution.py:25
  31.0 14.2 %collective-permute-start.7 = (f32[1,64,512]{2,1,0:T(8,128)}, f32[1,64,512]{2,1,0:T(8,128)}, u32[]{:S(2)}, u32[]{:S(2)}) collective-permute-start(f32[1,64,512]{2,1,0:T(8,128)} %add_add_fusion.1), channel_id=1, source_target_pairs={{0,2},{1,3},{2,0},{3,1},{4,6},{5,7},{6,4},{7,5},{8,10},{9,11},{10,... | collective-permute-start | bytes 393224 | tf_op jit(solution)/shard_map/ppermute | solution.py:25
  31.7 16.1 %collective-permute-start.14 = (f32[1,520,128]{2,1,0:T(8,128)}, f32[1,520,128]{2,1,0:T(8,128)}, u32[]{:S(2)}, u32[]{:S(2)}) collective-permute-start(f32[1,520,128]{2,1,0:T(8,128)} %add.103), channel_id=1, source_target_pairs={{0,24},{4,28},{8,16},{12,20},{16,8},{20,12},{24,0},{28,4},{1,25},{... | collective-permute-start | bytes 798728 | tf_op jit(solution)/shard_map/ppermute | solution.py:25
  33.3 18.5 %collective-permute-start.12 = (f32[1,520,128]{2,1,0:T(8,128)}, f32[1,520,128]{2,1,0:T(8,128)}, u32[]{:S(2)}, u32[]{:S(2)}) collective-permute-start(f32[1,520,128]{2,1,0:T(8,128)} %add.102), channel_id=1, source_target_pairs={{0,16},{4,20},{8,24},{12,28},{16,0},{20,4},{24,8},{28,12},{1,17},{... | collective-permute-start | bytes 798728 | tf_op jit(solution)/shard_map/ppermute | solution.py:25
  34.0 10.1 %copy-start.5 = (f32[1024,64]{0,1:T(8,128)S(1)}, f32[1024,64]{0,1:T(8,128)}, u32[]{:S(2)}) copy-start(f32[1024,64]{0,1:T(8,128)} %param.13) | copy-start | bytes 786436
  34.1 17.7 %collective-permute-start.10 = (f32[1,520,128]{2,1,0:T(8,128)S(1)}, f32[1,520,128]{2,1,0:T(8,128)S(1)}, u32[]{:S(2)}, u32[]{:S(2)}) collective-permute-start(f32[1,520,128]{2,1,0:T(8,128)S(1)} %add.101), channel_id=1, source_target_pairs={{0,8},{4,12},{8,0},{12,4},{16,24},{20,28},{24,16},{28,20},{1,9},{5... | collective-permute-start | bytes 798728 | tf_op jit(solution)/shard_map/ppermute | solution.py:25
  37.6 15.5 %collective-permute-start.15 = (f32[1,64,1024]{2,1,0:T(8,128)S(1)}, f32[1,64,1024]{2,1,0:T(8,128)S(1)}, u32[]{:S(2)}, u32[]{:S(2)}) collective-permute-start(f32[1,64,1024]{2,1,0:T(8,128)S(1)} %get-tuple-element.59), channel_id=1, source_target_pairs={{0,2},{1,3},{2,0},{3,1},{4,6},{5,7},{6,4},{7,5},{8,10},{9,11},{10,... | collective-permute-start | bytes 786440 | tf_op jit(solution)/shard_map/ppermute | solution.py:25
  44.1 9.0 %copy-start.4 = (f32[513,128]{1,0:T(8,128)S(1)}, f32[513,128]{1,0:T(8,128)}, u32[]{:S(2)}) copy-start(f32[513,128]{1,0:T(8,128)} %old_ref.1) | copy-start | bytes 787972
  46.2 11.8 %copy-start.1 = (f32[512,512]{1,0:T(8,128)S(1)}, f32[512,512]{1,0:T(8,128)}, u32[]{:S(2)}) copy-start(f32[512,512]{1,0:T(8,128)} %old_ref.2) | copy-start | bytes 3145732
  46.2 8.8 %collective-permute-start.18 = (f32[1,64,512]{2,1,0:T(8,128)S(1)}, f32[1,64,512]{2,1,0:T(8,128)S(1)}, u32[]{:S(2)}, u32[]{:S(2)}) collective-permute-start(f32[1,64,512]{2,1,0:T(8,128)S(1)} %add_add_fusion.refs_0_), channel_id=1, source_target_pairs={{0,24},{4,28},{8,16},{12,20},{16,8},{20,12},{24,0},{28,4},{1,25},{... | collective-permute-start | bytes 393224 | tf_op jit(solution)/shard_map/ppermute | solution.py:25
  47.9 7.8 %collective-permute-start.17 = (f32[1,64,512]{2,1,0:T(8,128)S(1)}, f32[1,64,512]{2,1,0:T(8,128)S(1)}, u32[]{:S(2)}, u32[]{:S(2)}) collective-permute-start(f32[1,64,512]{2,1,0:T(8,128)S(1)} %add_add_fusion.refs_0_), channel_id=1, source_target_pairs={{0,16},{4,20},{8,24},{12,28},{16,0},{20,4},{24,8},{28,12},{1,17},{... | collective-permute-start | bytes 393224 | tf_op jit(solution)/shard_map/ppermute | solution.py:25
  51.7 5.0 %collective-permute-start.16 = (f32[1,64,512]{2,1,0:T(8,128)S(1)}, f32[1,64,512]{2,1,0:T(8,128)S(1)}, u32[]{:S(2)}, u32[]{:S(2)}) collective-permute-start(f32[1,64,512]{2,1,0:T(8,128)S(1)} %add_add_fusion.refs_0_), channel_id=1, source_target_pairs={{0,8},{4,12},{8,0},{12,4},{16,24},{20,28},{24,16},{28,20},{1,9},{5... | collective-permute-start | bytes 393224 | tf_op jit(solution)/shard_map/ppermute | solution.py:25
  51.8 5.0 %collective-permute-start.19 = (f32[1,64,512]{2,1,0:T(8,128)S(1)}, f32[1,64,512]{2,1,0:T(8,128)S(1)}, u32[]{:S(2)}, u32[]{:S(2)}) collective-permute-start(f32[1,64,512]{2,1,0:T(8,128)S(1)} %add_add_fusion.refs_0_), channel_id=1, source_target_pairs={{0,4},{4,0},{8,12},{12,8},{16,20},{20,16},{24,28},{28,24},{1,5},{5... | collective-permute-start | bytes 393224 | tf_op jit(solution)/shard_map/ppermute | solution.py:25
  55.0 1.8 %collective-permute-start.22 = (f32[1,64,512]{2,1,0:T(8,128)S(1)}, f32[1,64,512]{2,1,0:T(8,128)S(1)}, u32[]{:S(2)}, u32[]{:S(2)}) collective-permute-start(f32[1,64,512]{2,1,0:T(8,128)S(1)} %collective-permute-done.18.refs_3_), channel_id=1, source_target_pairs={{0,4},{4,0},{8,12},{12,8},{16,20},{20,16},{24,28},{28,24},{1,5},{5... | collective-permute-start | bytes 393224 | tf_op jit(solution)/shard_map/ppermute | solution.py:25
  55.7 1.3 %collective-permute-start.21 = (f32[1,64,512]{2,1,0:T(8,128)S(1)}, f32[1,64,512]{2,1,0:T(8,128)S(1)}, u32[]{:S(2)}, u32[]{:S(2)}) collective-permute-start(f32[1,64,512]{2,1,0:T(8,128)S(1)} %collective-permute-done.17.refs_2_), channel_id=1, source_target_pairs={{0,4},{4,0},{8,12},{12,8},{16,20},{20,16},{24,28},{28,24},{1,5},{5... | collective-permute-start | bytes 393224 | tf_op jit(solution)/shard_map/ppermute | solution.py:25
  56.7 1.3 %collective-permute-start.20 = (f32[1,64,512]{2,1,0:T(8,128)S(1)}, f32[1,64,512]{2,1,0:T(8,128)S(1)}, u32[]{:S(2)}, u32[]{:S(2)}) collective-permute-start(f32[1,64,512]{2,1,0:T(8,128)S(1)} %collective-permute-done.16.refs_1_), channel_id=1, source_target_pairs={{0,4},{4,0},{8,12},{12,8},{16,20},{20,16},{24,28},{28,24},{1,5},{5... | collective-permute-start | bytes 393224 | tf_op jit(solution)/shard_map/ppermute | solution.py:25

commit v3 on v2

--- a/solution.py
+++ b/solution.py
@@ -10,9 +10,11 @@
 
 F32 = jnp.float32
 RADIX = 4
-CHUNKS = 4
+CHUNKS = 2
 DIRECT = True
 VMEM_LIMIT = 8 * 1024 * 1024
+LAST = pl.CostEstimate(flops=10**6, bytes_accessed=1024 * 1024, transcendentals=0)
+LITTLE = pl.CostEstimate(flops=10**6, bytes_accessed=1024, transcendentals=0)
 BESIDE = pl.CostEstimate(flops=10**11, bytes_accessed=4 * 1024 * 1024, transcendentals=0)
 FIRST_LIMIT = 60 * 1024 * 1024
 
@@ -33,21 +35,22 @@
     return pl.BlockSpec(shape, lambda i, at: (0,) * len(shape))
 
 
-def core_kernel(
-    parts, other, phi_any, metric_any, theta_any,
-    out_ref, phi, metric, theta, high, low, sum_ref, sems,
+def first_kernel(
+    parts, phi_any, metric_any, theta_any, omega_any,
+    send_ref, keep_ref, near_ref, far_ref, own_ref,
+    phi, metric, theta, omega, high, low, sum_ref, range_ref, sems,
 ):
-    me = lax.axis_index("series")
+    me, slot = lax.axis_index("series"), lax.axis_index("tm")
     core, chip = me & 1, me >> 1
-    rows, cols = phi.shape[0], metric.shape[1] // CHUNKS
-    first = pl.multiple_of((core ^ other) * rows, rows)
-    copies = [pltpu.make_async_copy(phi_any.at[pl.ds(first, rows), :], phi, sems.at[0])]
+    cols = metric.shape[1] // CHUNKS
+    copies = [pltpu.make_async_copy(phi_any, phi, sems.at[0])]
     for c in range(CHUNKS):
         at = slice(c * cols, (c + 1) * cols)
         copies.append(
             pltpu.make_async_copy(metric_any.at[:, at], metric.at[:, at], sems.at[1 + c])
         )
     copies.append(pltpu.make_async_copy(theta_any, theta, sems.at[1 + CHUNKS]))
+    copies.append(pltpu.make_async_copy(omega_any, omega, sems.at[2 + CHUNKS]))
     for copy in copies:
         copy.start()
     copies[0].wait()
@@ -58,73 +61,62 @@
         top = left.astype(jnp.bfloat16)
         high[:, at] = top
         low[:, at] = (left - top.astype(F32)).astype(jnp.bfloat16)
+    copies[-2].wait()
     copies[-1].wait()
     by_rows = (((1,), (1,)), ((), ()))
     sum_ref[...] = lax.dot_general(high[...], theta[...], by_rows, preferred_element_type=F32)
     sum_ref[...] += lax.dot_general(low[...], theta[...], by_rows, preferred_element_type=F32)
-    block = rows // parts
-    for k in range(parts):
-        out_ref[k] = sum_ref[pl.ds(pl.multiple_of((chip ^ k) * block, block), block), :]
-
-
-def core_half(other, phi, metric, theta, parts):
+    half = sum_ref.shape[0] // 2
+    rows = half // parts
+    for ref, side in ((send_ref, 1 - core), (keep_ref, core)):
+        for k in range(parts):
+            first = pl.multiple_of(side * half + (chip ^ k) * rows, rows)
+            ref[k] = sum_ref[pl.ds(first, rows), :]
+    range_ref[...] = lax.dot_general(
+        omega[...], metric[...], (((0,), (1,)), ((), ())), preferred_element_type=F32
+    )
+    width = own_ref.shape[0]
+
+    def block(k):
+        return range_ref[pl.ds(pl.multiple_of((slot ^ k) * width, width), width), :]
+
+    for j in range(near_ref.shape[0]):
+        near_ref[j] = block(2 * j + 1)
+    for j in range(far_ref.shape[0]):
+        far_ref[j] = block(2 * j + 2)
+    own_ref[...] = block(0)
+
+
+def first_products(phi, metric, theta, omega, parts, slots):
     order, depth = phi.shape
-    rows, cols = order // 2, theta.shape[0]
-    left = (rows, metric.shape[1])
-    shape = (parts, rows // parts, cols)
-    return pl.pallas_call(
-        functools.partial(core_kernel, parts, other),
-        in_specs=[pl.BlockSpec(memory_space=pl.ANY)] * 3,
-        out_specs=pl.BlockSpec(memory_space=pltpu.VMEM),
+    cols, series, width = theta.shape[0], metric.shape[0], omega.shape[1]
+    rows, block = order // 2 // parts, width // slots
+    shapes = [(parts, rows, cols)] * 2
+    shapes += [(slots // 2, block, series), (slots // 2 - 1, block, series), (block, series)]
+    return pl.pallas_call(
+        functools.partial(first_kernel, parts),
+        in_specs=[pl.BlockSpec(memory_space=pl.ANY)] * 4,
+        out_specs=[pl.BlockSpec(memory_space=pltpu.VMEM)] * len(shapes),
         scratch_shapes=[
-            pltpu.VMEM((rows, depth), phi.dtype),
+            pltpu.VMEM(phi.shape, phi.dtype),
             pltpu.VMEM(metric.shape, metric.dtype),
             pltpu.VMEM(theta.shape, theta.dtype),
-            pltpu.VMEM(left, jnp.bfloat16),
-            pltpu.VMEM(left, jnp.bfloat16),
-            pltpu.VMEM((rows, cols), F32),
-            pltpu.SemaphoreType.DMA((CHUNKS + 2,)),
+            pltpu.VMEM(omega.shape, omega.dtype),
+            pltpu.VMEM((order, metric.shape[1]), jnp.bfloat16),
+            pltpu.VMEM((order, metric.shape[1]), jnp.bfloat16),
+            pltpu.VMEM((order, cols), F32),
+            pltpu.VMEM((width, series), F32),
+            pltpu.SemaphoreType.DMA((CHUNKS + 3,)),
         ],
-        out_shape=jax.ShapeDtypeStruct(shape, F32),
+        out_shape=[jax.ShapeDtypeStruct(s, F32) for s in shapes],
         compiler_params=pltpu.CompilerParams(vmem_limit_bytes=FIRST_LIMIT),
-        name="core_half",
-    )(phi, metric, theta)
-
-
-def range_kernel(parts, at_ref, omega_ref, metric_ref, send_ref, far_ref, own_ref, sum_ref):
-    slot = at_ref[0]
-    sum_ref[...] = lax.dot_general(
-        omega_ref[...], metric_ref[...], (((0,), (1,)), ((), ())), preferred_element_type=F32
-    )
-    rows = sum_ref.shape[0] // parts
-
-    def block(k):
-        return sum_ref[pl.ds(pl.multiple_of((slot ^ k) * rows, rows), rows), :]
-
-    for j in range(parts // 2):
-        send_ref[j] = block(2 * j + 1)
-    for j in range(1, parts // 2):
-        far_ref[j - 1] = block(2 * j)
-    own_ref[...] = block(0)
-
-
-def range_blocks(slot, omega, metric, parts):
-    series, width = metric.shape[0], omega.shape[1]
-    rows = width // parts
-    shapes = [(parts // 2, rows, series), (parts // 2 - 1, rows, series), (rows, series)]
-    return pl.pallas_call(
-        functools.partial(range_kernel, parts),
-        grid_spec=pltpu.PrefetchScalarGridSpec(
-            num_scalar_prefetch=1,
-            grid=(1,),
-            in_specs=[whole(omega.shape), whole(metric.shape)],
-            out_specs=[whole(s) for s in shapes],
-            scratch_shapes=[pltpu.VMEM((width, series), F32)],
+        cost_estimate=pl.CostEstimate(
+            flops=2 * depth * metric.shape[1] * (order + width) + 4 * order * cols * metric.shape[1],
+            bytes_accessed=4 * 1024 * 1024,
+            transcendentals=0,
         ),
-        out_shape=[jax.ShapeDtypeStruct(s, F32) for s in shapes],
-        compiler_params=params(),
-        name="range_blocks",
-    )(jnp.stack([slot]), omega, metric)
+        name="first_products",
+    )(phi, metric, theta, omega)
 
 
 def corange_kernel(parts, at_ref, psi_ref, metric_ref, *refs):
@@ -172,59 +164,56 @@
     return blocks[:radix], blocks[radix:]
 
 
-def range_add_kernel(own_ref, far_ref, got_ref, own_out, far_out):
-    own_out[...] = own_ref[...] + got_ref[0]
-    far_out[...] = far_ref[...] + got_ref[1:]
-
-
-def range_add(own, far, got):
+def near_add_kernel(old_ref, own_ref, got_ref, out_ref):
+    out_ref[...] = old_ref[...] + (own_ref[...] + got_ref[0])
+
+
+def near_add(old, own, got):
     vmem = pl.BlockSpec(memory_space=pltpu.VMEM)
     return pl.pallas_call(
-        range_add_kernel,
+        near_add_kernel,
         in_specs=[vmem] * 3,
-        out_specs=[vmem] * 2,
-        out_shape=[jax.ShapeDtypeStruct(a.shape, F32) for a in (own, far)],
-        compiler_params=params(),
-        cost_estimate=BESIDE,
-        name="range_add",
-    )(own, far, got)
-
-
-def base_add_kernel(old_ref, own_ref, out_ref):
-    out_ref[...] = old_ref[...] + own_ref[...]
-
-
-def base_add(old, own):
-    vmem = pl.BlockSpec(memory_space=pltpu.VMEM)
-    return pl.pallas_call(
-        base_add_kernel,
-        in_specs=[vmem] * 2,
         out_specs=vmem,
         out_shape=jax.ShapeDtypeStruct(old.shape, F32),
         compiler_params=params(),
         cost_estimate=BESIDE,
-        name="base_add",
-    )(old, own)
-
-
-def last_add_kernel(count, old_ref, base_ref, *refs):
+        name="near_add",
+    )(old, own, got)
+
+
+def far_add_kernel(far_ref, got_ref, out_ref):
+    out_ref[...] = far_ref[...] + got_ref[1:]
+
+
+def far_add(far, got):
+    vmem = pl.BlockSpec(memory_space=pltpu.VMEM)
+    return pl.pallas_call(
+        far_add_kernel,
+        in_specs=[vmem] * 2,
+        out_specs=vmem,
+        out_shape=jax.ShapeDtypeStruct(far.shape, F32),
+        compiler_params=params(),
+        cost_estimate=LITTLE,
+        name="far_add",
+    )(far, got)
+
+
+def corange_add_kernel(old_ref, *refs):
     rows = old_ref.shape[0]
-    corange_out, range_out = refs[-2:]
-    corange_out[...] = old_ref[...] + added([r[0, :rows] for r in refs[:count]])
-    range_out[...] = base_ref[...] + added([r[0] for r in refs[count:-2]])
-
-
-def last_add(old, terms, base, got):
+    refs[-1][...] = old_ref[...] + added([r[0, :rows] for r in refs[:-1]])
+
+
+def corange_add(old, terms):
     vmem = pl.BlockSpec(memory_space=pltpu.VMEM)
     return pl.pallas_call(
-        functools.partial(last_add_kernel, len(terms)),
-        in_specs=[vmem] * (2 + len(terms) + len(got)),
-        out_specs=[vmem] * 2,
-        out_shape=[jax.ShapeDtypeStruct(a.shape, F32) for a in (old, base)],
+        corange_add_kernel,
+        in_specs=[vmem] * (1 + len(terms)),
+        out_specs=vmem,
+        out_shape=jax.ShapeDtypeStruct(old.shape, F32),
         compiler_params=params(),
-        cost_estimate=BESIDE,
-        name="last_add",
-    )(old, base, *terms, *got)
+        cost_estimate=LAST,
+        name="corange_add",
+    )(old, *terms)
 
 
 def place_kernel(rows, half, radix, at_ref, old_ref, *refs):
@@ -298,22 +287,27 @@
     core, chip = me & 1, me >> 1
     chips = series // 2
 
-    core_send = core_half(1, phi, metric, theta, chips)
+    core_send, core_keep, near, far, own = first_products(phi, metric, theta, omega, chips, tm)
     core_got = swap(core_send, "series", 1, series)
-    core_keep = core_half(0, after(phi, core_send), metric, theta, chips)
+    range_got = swap(near, "tm", 1, tm)
     radix = min(RADIX, chips)
     core_terms = sum_over_chips([split(core_keep, radix), split(core_got, radix)], series)
 
-    near, far, own = range_blocks(slot, after(omega, core_terms[0]), metric, tm)
-    range_got = swap(near, "tm", 1, tm)
-    corange_send, corange_keep = corange_blocks(core, chip, after(psi, near), metric, chips)
+    corange_send, corange_keep = corange_blocks(core, chip, after(psi, core_terms[0]), metric, chips)
     corange_got = [swap(b, "series", 1, series) for b in corange_send]
     corange_terms = sum_over_chips([corange_keep, corange_got], series)
 
     core_part = added([after(t, *corange_send) for t in core_terms])
-    parts = [core_part] + [swap(core_part, "tm", k, tm) for k in range(1, tm)]
-
-    own, far = range_add(own, after(far, core_part, corange_terms[0]), range_got)
+
+    got = swap(core_part, "tm", 1, tm)
+    base = near_add(range_old.T, after(own, core_part, corange_terms[0]), range_got)
+    core_all = core_part + after(got, base)
+    distance = 2
+    while distance < tm:
+        core_all = core_all + swap(core_all, "tm", distance, tm)
+        distance *= 2
+
+    far = far_add(after(far, core_all), range_got)
     late = []
     distance = 2
     while distance < tm:
@@ -321,19 +315,14 @@
         late.append(got[:1])
         far = far[1::2] + got[1:]
         distance *= 2
-    base = base_add(range_old.T, own)
-
-    parts = [after(p, base) for p in parts]
-    while len(parts) > 1:
-        parts = [a + b for a, b in zip(parts[::2], parts[1::2])]
-    core_all = parts[0]
-
-    corange_new, range_new = last_add(after(corange_old, core_all), corange_terms, base, late)
+
+    corange_new = corange_add(after(corange_old, core_all), corange_terms)
     pieces = gather_over_chips(core_all, series)
     pieces = pieces[:1] + [after(p, corange_new) for p in pieces[1:]]
     pieces = pieces + [swap(p, "series", 1, series) for p in pieces]
     core_new = placed(core, chip, core_old, pieces, chips)
-    return range_new.T, corange_new, core_new
+    range_new = (base + added([g[0] for g in late])).T
+    return range_new, corange_new, core_new
 
 
 def solution(mesh):

time: 59.9 us -> 53.1 us (0.89)
  starting transfers between devices: 27.3 us -> 19 us
  waiting for transfers between devices: 11.2 us -> 19 us
  Pallas kernels: 15.7 us -> 10.6 us
  other arithmetic: 4.65 us -> 2.29 us
  local copies, waits for them, and re-layouts: 0.02 us -> 1.27 us
    ppermute x23 -> x22, starting transfers between devices: 27.3 us -> 19 us  [swap(): return lax.ppermute(value, axis, [(i, i ^ bits) for i in range(size)])]
    ppermute x23 -> x22, waiting for transfers between devices: 11.2 us -> 19 us  [swap(): return lax.ppermute(value, axis, [(i, i ^ bits) for i in range(size)])]
    pallas_call x6 -> x4, Pallas kernels: 12 us -> 6.96 us  [the longest x1 6.04 us: first_products(): pl.pallas_call(functools.partial(first_kernel, parts), in_specs=[pl.Block...]
    add x6, other arithmetic: 3.49 us -> 1.36 us  [added(): return functools.reduce(operator.add, terms)]
    unnamed x12 -> x14, local copies, waits for them, and re-layouts: 0.02 us -> 1.27 us
    add x1 -> x2, other arithmetic: 1.01 us -> 0.04 us  [the longest x1 0.02 us: body(): core_all = core_part + after(got, base)]
    transpose x0 -> x1, other arithmetic: none -> 0.74 us  [body(): range_new = (base + added([g[0] for g in late])).T]
  transfers between devices with their start and end apart: 23 -> 22, of which waited for: 9 -> 9; matrix products, arithmetic and copies ran while one was open for 6% -> 4% of each run, Pallas kernels for 15% -> 6%
where the time goes in v3:
time: 53.1 us; the launch traced here: 52.9 us
  starting transfers between devices  19 us (36%)
  waiting for transfers between devices  19 us (36%)
  Pallas kernels  10.6 us (20%)
  other arithmetic  2.29 us (4%)
  local copies, waits for them, and re-layouts  1.27 us (2%)
  between operations  0.82 us (2%)
    ppermute x22, starting transfers between devices, swap(): return lax.ppermute(value, axis, [(i, i ^ bits) for i in range(size)])  19 us
    ppermute x22, waiting for transfers between devices, swap(): return lax.ppermute(value, axis, [(i, i ^ bits) for i in range(size)])  19 us
    pallas_call x1, Pallas kernels, first_products(): pl.pallas_call(functools.partial(first_kernel, parts), in_specs=[pl.Block...  6.04 us
    pallas_call x1, Pallas kernels, corange_blocks(): pl.pallas_call(functools.partial(corange_kernel, parts), grid_spec=pltpu....  2.03 us
    pallas_call x1, Pallas kernels, placed(): pl.pallas_call(functools.partial(place_kernel, rows, parts, len(pieces) /...  1.63 us
    add x6, other arithmetic, added(): return functools.reduce(operator.add, terms)  1.36 us
    unnamed x14, local copies, waits for them, and re-layouts  1.27 us
  transfers between devices with their start and end apart: 22, of which 9 were waited for; matrix products, arithmetic and copies ran while one was open for 4% of the time, Pallas kernels for 6%

profile of v3, /device:TPU:0, one launch (start us, length us, event | category | flops | bytes accessed | tf_op | source)
XLA Modules:
  0.0 52.9 jit_solution(5199949526957947369)
XLA Ops:
  0.6 6.0 %first_products.1 = (f32[4,64,512]{2,1,0:T(8,128)}, f32[4,64,512]{2,1,0:T(8,128)}, f32[2,64,1024]{2,1,0:T(8,128)}, f32[1,64,1024]{2,1,0:T(8,128)}, f32[64,1024]{1,0:T(8,128)}) custom-call(bf16[512,1024]{1,0:T(8,128)(2,1)} %phi_any.1, bf16[1024,1024]{1,0:T(8,128)(2,1)} %metric_ref.1, bf16[512,1024]{1,0:T(8,128)(2,1)} %theta_any.1, bf16[1024,256]{1,0:T(8,128)(2,1)} %omega_any.1), custom_call_target="tpu_custom_call" | custom-call | flops 2684354560 | bytes 4194304 | tf_op jit(solution)/shard_map/first_products/pallas_call | solution.py:96
  6.7 0.5 collective-permute-start
  7.2 2.7 %collective-permute-start.5 = (f32[2,64,1024]{2,1,0:T(8,128)}, f32[2,64,1024]{2,1,0:T(8,128)S(1)}, u32[]{:S(2)}, u32[]{:S(2)}) collective-permute-start(f32[2,64,1024]{2,1,0:T(8,128)} %get-tuple-element.42), channel_id=1, source_target_pairs={{0,1},{1,0},{2,3},{3,2},{4,5},{5,4},{6,7},{7,6},{8,9},{9,8},{10,11... | collective-permute-start | bytes 1572872 | tf_op jit(solution)/shard_map/ppermute | solution.py:27
  9.9 0.1 pad_add_fusion.at_ref
  9.9 1.2 %fusion.3 = (f32[1,64,512]{2,1,0:T(8,128)S(1)}, f32[1,64,512]{2,1,0:T(8,128)S(1)}, f32[1,64,512]{2,1,0:T(8,128)S(1)}, f32[1,64,512]{2,1,0:T(8,128)S(1)}) fusion(f32[1,4,64,512]{3,2,1,0:T(8,128)S(1)} %bitcast.21, f32[1,4,64,512]{3,2,1,0:T(8,128)} %bitcast.20), kind=kLoop, calls=%fused_computation.7 | loop fusion | flops 131072 | bytes 1572864 | tf_op jit(solution)/shard_map/add | solution.py:23
  11.1 1.9 %collective-permute-start.1 = (f32[1,64,512]{2,1,0:T(8,128)S(1)}, f32[1,64,512]{2,1,0:T(8,128)S(1)}, u32[]{:S(2)}, u32[]{:S(2)}) collective-permute-start(f32[1,64,512]{2,1,0:T(8,128)S(1)} %get-tuple-element.53), channel_id=1, source_target_pairs={{0,8},{4,12},{8,0},{12,4},{16,24},{20,28},{24,16},{28,20},{1,9},{5... | collective-permute-start | bytes 393224 | tf_op jit(solution)/shard_map/ppermute | solution.py:27
  13.1 1.5 %collective-permute-start.3 = (f32[1,64,512]{2,1,0:T(8,128)S(1)}, f32[1,64,512]{2,1,0:T(8,128)S(1)}, u32[]{:S(2)}, u32[]{:S(2)}) collective-permute-start(f32[1,64,512]{2,1,0:T(8,128)S(1)} %get-tuple-element.54), channel_id=1, source_target_pairs={{0,24},{4,28},{8,16},{12,20},{16,8},{20,12},{24,0},{28,4},{1,25},{... | collective-permute-start | bytes 393224 | tf_op jit(solution)/shard_map/ppermute | solution.py:27
  14.5 0.1 collective-permute-start.2
  14.7 1.2 %copy-done.4 = bf16[513,1024]{1,0:T(8,128)(2,1)S(1)} copy-done((bf16[513,1024]{1,0:T(8,128)(2,1)S(1)}, bf16[513,1024]{1,0:T(8,128)(2,1)}, u32[]{:S(2)}) %copy-start.4) | copy-done | bytes 1050648
  15.9 2.0 %corange_blocks.1 = (f32[1,520,128]{2,1,0:T(8,128)S(1)}, f32[1,520,128]{2,1,0:T(8,128)S(1)}, f32[1,520,128]{2,1,0:T(8,128)S(1)}, f32[1,520,128]{2,1,0:T(8,128)S(...) custom-call(s32[2]{0:T(128)S(1)} %pad_add_fusion.at_ref, ...), custom_call_target="tpu_custom_call" | custom-call | flops 99999997952 | bytes 4194304 | tf_op jit(solution)/shard_map/corange_blocks/pallas_call | solution.py:150
  17.9 0.0 copy-start.5
  18.0 0.0 copy-start.6
  18.0 0.1 collective-permute-start.4
  18.0 2.9 %collective-permute-done.3 = f32[1,64,512]{2,1,0:T(8,128)S(1)} collective-permute-done((f32[1,64,512]{2,1,0:T(8,128)S(1)}, f32[1,64,512]{2,1,0:T(8,128)S(1)}, u32[]{:S(2)}, u32[]{:S(2)}) %collective-permute-start.3) | collective-permute-done | bytes 131104 | tf_op jit(solution)/shard_map/ppermute | solution.py:27
  21.0 1.4 %collective-permute-done.2 = f32[1,64,512]{2,1,0:T(8,128)S(1)} collective-permute-done((f32[1,64,512]{2,1,0:T(8,128)S(1)}, f32[1,64,512]{2,1,0:T(8,128)S(1)}, u32[]{:S(2)}, u32[]{:S(2)}) %collective-permute-start.2) | collective-permute-done | bytes 131104 | tf_op jit(solution)/shard_map/ppermute | solution.py:27
  22.3 0.0 collective-permute-start.11
  22.3 0.0 collective-permute-done.1
  22.3 0.5 collective-permute-start.13
  22.9 1.6 %collective-permute-start.6 = (f32[1,64,512]{2,1,0:T(8,128)S(1)}, f32[1,64,512]{2,1,0:T(8,128)S(1)}, u32[]{:S(2)}, u32[]{:S(2)}) collective-permute-start(f32[1,64,512]{2,1,0:T(8,128)S(1)} %add_add_fusion), channel_id=1, source_target_pairs={{0,1},{1,0},{2,3},{3,2},{4,5},{5,4},{6,7},{7,6},{8,9},{9,8},{10,11... | collective-permute-start | bytes 393224 | tf_op jit(solution)/shard_map/ppermute | solution.py:27
  24.6 0.0 collective-permute-done.9
  24.6 1.6 %collective-permute-start.10 = (f32[1,520,128]{2,1,0:T(8,128)S(1)}, f32[1,520,128]{2,1,0:T(8,128)S(1)}, u32[]{:S(2)}, u32[]{:S(2)}) collective-permute-start(f32[1,520,128]{2,1,0:T(8,128)S(1)} %add.101), channel_id=1, source_target_pairs={{0,8},{4,12},{8,0},{12,4},{16,24},{20,28},{24,16},{28,20},{1,9},{5... | collective-permute-start | bytes 798728 | tf_op jit(solution)/shard_map/ppermute | solution.py:27
  26.2 0.6 %collective-permute-start.12 = (f32[1,520,128]{2,1,0:T(8,128)S(1)}, f32[1,520,128]{2,1,0:T(8,128)S(1)}, u32[]{:S(2)}, u32[]{:S(2)}) collective-permute-start(f32[1,520,128]{2,1,0:T(8,128)S(1)} %add.102), channel_id=1, source_target_pairs={{0,16},{4,20},{8,24},{12,28},{16,0},{20,4},{24,8},{28,12},{1,17},{... | collective-permute-start | bytes 798728 | tf_op jit(solution)/shard_map/ppermute | solution.py:27
  26.8 0.0 collective-permute-done.5.got_ref
  26.8 0.0 copy-start.2
  26.8 0.1 near_add.1
  26.9 0.0 copy-start.1
  26.9 1.5 %collective-permute-done.6 = f32[1,64,512]{2,1,0:T(8,128)S(1)} collective-permute-done((f32[1,64,512]{2,1,0:T(8,128)S(1)}, f32[1,64,512]{2,1,0:T(8,128)S(1)}, u32[]{:S(2)}, u32[]{:S(2)}) %collective-permute-start.6) | collective-permute-done | bytes 131104 | tf_op jit(solution)/shard_map/ppermute | solution.py:27
  28.4 2.7 %collective-permute-start.7 = (f32[1,64,512]{2,1,0:T(8,128)S(1)}, f32[1,64,512]{2,1,0:T(8,128)S(1)}, u32[]{:S(2)}, u32[]{:S(2)}) collective-permute-start(f32[1,64,512]{2,1,0:T(8,128)S(1)} %add.98), channel_id=1, source_target_pairs={{0,2},{1,3},{2,0},{3,1},{4,6},{5,7},{6,4},{7,5},{8,10},{9,11},{10,... | collective-permute-start | bytes 393224 | tf_op jit(solution)/shard_map/ppermute | solution.py:27
  31.1 0.0 collective-permute-done.13
  31.1 0.0 copy-start
  31.1 1.5 %collective-permute-start.14 = (f32[1,520,128]{2,1,0:T(8,128)S(1)}, f32[1,520,128]{2,1,0:T(8,128)S(1)}, u32[]{:S(2)}, u32[]{:S(2)}) collective-permute-start(f32[1,520,128]{2,1,0:T(8,128)S(1)} %add.103), channel_id=1, source_target_pairs={{0,24},{4,28},{8,16},{12,20},{16,8},{20,12},{24,0},{28,4},{1,25},{... | collective-permute-start | bytes 798728 | tf_op jit(solution)/shard_map/ppermute | solution.py:27
  32.6 4.1 %collective-permute-done.7 = f32[1,64,512]{2,1,0:T(8,128)S(1)} collective-permute-done((f32[1,64,512]{2,1,0:T(8,128)S(1)}, f32[1,64,512]{2,1,0:T(8,128)S(1)}, u32[]{:S(2)}, u32[]{:S(2)}) %collective-permute-start.7) | collective-permute-done | bytes 131104 | tf_op jit(solution)/shard_map/ppermute | solution.py:27
  36.8 0.3 collective-permute-start.8
  37.1 1.4 %collective-permute-start.17 = (f32[1,64,512]{2,1,0:T(8,128)S(1)}, f32[1,64,512]{2,1,0:T(8,128)S(1)}, u32[]{:S(2)}, u32[]{:S(2)}) collective-permute-start(f32[1,64,512]{2,1,0:T(8,128)S(1)} %add.99.refs_0_), channel_id=1, source_target_pairs={{0,24},{4,28},{8,16},{12,20},{16,8},{20,12},{24,0},{28,4},{1,25},{... | collective-permute-start | bytes 393224 | tf_op jit(solution)/shard_map/ppermute | solution.py:27
  38.5 0.0 collective-permute-done.10.refs_1_
  38.5 1.5 %collective-permute-start.16 = (f32[1,64,512]{2,1,0:T(8,128)S(1)}, f32[1,64,512]{2,1,0:T(8,128)S(1)}, u32[]{:S(2)}, u32[]{:S(2)}) collective-permute-start(f32[1,64,512]{2,1,0:T(8,128)S(1)} %add.99.refs_0_), channel_id=1, source_target_pairs={{0,16},{4,20},{8,24},{12,28},{16,0},{20,4},{24,8},{28,12},{1,17},{... | collective-permute-start | bytes 393224 | tf_op jit(solution)/shard_map/ppermute | solution.py:27
  40.0 1.4 %collective-permute-done.12.refs_2_ = f32[1,520,128]{2,1,0:T(8,128)S(1)} collective-permute-done((f32[1,520,128]{2,1,0:T(8,128)S(1)}, f32[1,520,128]{2,1,0:T(8,128)S(1)}, u32[]{:S(2)}, u32[]{:S(2)}) %collective-permute-start.12) | collective-permute-done | bytes 266272 | tf_op jit(solution)/shard_map/ppermute | solution.py:27
  41.4 0.1 pad_add_fusion.1.at_ref
  41.5 0.0 collective-permute-start.18
  41.6 0.8 %corange_add.1 = f32[513,128]{1,0:T(8,128)} custom-call(f32[513,128]{1,0:T(8,128)S(1)} %copy-done.1, f32[1,520,128]{2,1,0:T(8,128)S(1)} %add.97.refs_0_, f32[1,520,128]{2,1,0:T(8,128)S(1)} %collective-permute-done.10.refs_1_, f32[1,520,128]{2,1,0:T(8,128)S(1)} %collective-permute-done.12.refs_2_, f32[1,520,128]{2,1,0:T(8,128)S(1)} %collective-permute-done.14.refs_3_), custom_call_target="tpu_custom_call" | custom-call | flops 1000000 | bytes 1048576 | tf_op jit(solution)/shard_map/corange_add/pallas_call | solution.py:208
  42.4 1.3 %collective-permute-done.17.refs_3_ = f32[1,64,512]{2,1,0:T(8,128)S(1)} collective-permute-done((f32[1,64,512]{2,1,0:T(8,128)S(1)}, f32[1,64,512]{2,1,0:T(8,128)S(1)}, u32[]{:S(2)}, u32[]{:S(2)}) %collective-permute-start.17) | collective-permute-done | bytes 131104 | tf_op jit(solution)/shard_map/ppermute | solution.py:27
  43.7 1.7 %collective-permute-done.16.refs_2_ = f32[1,64,512]{2,1,0:T(8,128)S(1)} collective-permute-done((f32[1,64,512]{2,1,0:T(8,128)S(1)}, f32[1,64,512]{2,1,0:T(8,128)S(1)}, u32[]{:S(2)}, u32[]{:S(2)}) %collective-permute-start.16) | collective-permute-done | bytes 131104 | tf_op jit(solution)/shard_map/ppermute | solution.py:27
  45.4 1.0 %collective-permute-done.15.refs_1_ = f32[1,64,512]{2,1,0:T(8,128)S(1)} collective-permute-done((f32[1,64,512]{2,1,0:T(8,128)S(1)}, f32[1,64,512]{2,1,0:T(8,128)S(1)}, u32[]{:S(2)}, u32[]{:S(2)}) %collective-permute-start.15) | collective-permute-done | bytes 131104 | tf_op jit(solution)/shard_map/ppermute | solution.py:27
  46.4 0.5 collective-permute-start.20
  46.9 0.0 collective-permute-start.21
  46.9 3.6 %collective-permute-done.8 = f32[1,64,1024]{2,1,0:T(8,128)S(1)} collective-permute-done((f32[1,64,1024]{2,1,0:T(8,128)S(1)}, f32[1,64,1024]{2,1,0:T(8,128)S(1)}, u32[]{:S(2)}, u32[]{:S(2)}) %collective-permute-start.8) | collective-permute-done | bytes 262176 | tf_op jit(solution)/shard_map/ppermute | solution.py:27
  50.5 0.7 %fusion = f32[1024,64]{0,1:T(8,128)} fusion(f32[64,1024]{1,0:T(8,128)S(1)} %near_add.1, f32[1,64,1024]{2,1,0:T(8,128)S(1)} %collective-permute-done.8), kind=kLoop, calls=%fused_computation.1 | loop fusion | flops 65536 | bytes 786432 | tf_op jit(solution)/shard_map/transpose | solution.py:324
  51.3 1.6 %placed.1 = f32[512,512]{1,0:T(8,128)} custom-call(s32[2]{0:T(128)S(1)} %pad_add_fusion.1.at_ref, f32[512,512]{1,0:T(8,128)S(1)} %copy-done, f32[1,64,512]{2,1,0:T(8,128)S(1)} %add.99.refs_0_, f32[1,64,512]{2,1,0:T(8,128)S(1)} %collective-permute-done.15.refs_1_, f32[1,64,512]{2,1,0:T(8,128)S(1)} %collective-permute-done.16.refs_2_, ...), custom_call_target="tpu_custom_call" | custom-call | tf_op jit(solution)/shard_map/placed/pallas_call | solution.py:232
  (27 shorter events, 0.3 us)
Async XLA Ops:
  0.6 14.0 %copy-start.3 = (bf16[1024,1024]{1,0:T(8,128)(2,1)S(1)}, bf16[1024,1024]{1,0:T(8,128)(2,1)}, u32[]{:S(2)}) copy-start(bf16[1024,1024]{1,0:T(8,128)(2,1)} %metric_ref.1) | copy-start | bytes 6291460
  6.7 3.2 %collective-permute-start = (f32[4,64,512]{2,1,0:T(8,128)}, f32[4,64,512]{2,1,0:T(8,128)S(1)}, u32[]{:S(2)}, u32[]{:S(2)}) collective-permute-start(f32[4,64,512]{2,1,0:T(8,128)} %get-tuple-element.30), channel_id=1, source_target_pairs={{0,4},{4,0},{8,12},{12,8},{16,20},{20,16},{24,28},{28,24},{1,5},{5... | collective-permute-start | bytes 1572872 | tf_op jit(solution)/shard_map/ppermute | solution.py:27
  7.2 19.6 %collective-permute-start.5 = (f32[2,64,1024]{2,1,0:T(8,128)}, f32[2,64,1024]{2,1,0:T(8,128)S(1)}, u32[]{:S(2)}, u32[]{:S(2)}) collective-permute-start(f32[2,64,1024]{2,1,0:T(8,128)} %get-tuple-element.42), channel_id=1, source_target_pairs={{0,1},{1,0},{2,3},{3,2},{4,5},{5,4},{6,7},{7,6},{8,9},{9,8},{10,11... | collective-permute-start | bytes 1572872 | tf_op jit(solution)/shard_map/ppermute | solution.py:27
  11.1 11.2 %collective-permute-start.1 = (f32[1,64,512]{2,1,0:T(8,128)S(1)}, f32[1,64,512]{2,1,0:T(8,128)S(1)}, u32[]{:S(2)}, u32[]{:S(2)}) collective-permute-start(f32[1,64,512]{2,1,0:T(8,128)S(1)} %get-tuple-element.53), channel_id=1, source_target_pairs={{0,8},{4,12},{8,0},{12,4},{16,24},{20,28},{24,16},{28,20},{1,9},{5... | collective-permute-start | bytes 393224 | tf_op jit(solution)/shard_map/ppermute | solution.py:27
  13.1 7.9 %collective-permute-start.3 = (f32[1,64,512]{2,1,0:T(8,128)S(1)}, f32[1,64,512]{2,1,0:T(8,128)S(1)}, u32[]{:S(2)}, u32[]{:S(2)}) collective-permute-start(f32[1,64,512]{2,1,0:T(8,128)S(1)} %get-tuple-element.54), channel_id=1, source_target_pairs={{0,24},{4,28},{8,16},{12,20},{16,8},{20,12},{24,0},{28,4},{1,25},{... | collective-permute-start | bytes 393224 | tf_op jit(solution)/shard_map/ppermute | solution.py:27
  14.5 7.8 %collective-permute-start.2 = (f32[1,64,512]{2,1,0:T(8,128)S(1)}, f32[1,64,512]{2,1,0:T(8,128)S(1)}, u32[]{:S(2)}, u32[]{:S(2)}) collective-permute-start(f32[1,64,512]{2,1,0:T(8,128)S(1)} %get-tuple-element.55), channel_id=1, source_target_pairs={{0,16},{4,20},{8,24},{12,28},{16,0},{20,4},{24,8},{28,12},{1,17},{... | collective-permute-start | bytes 393224 | tf_op jit(solution)/shard_map/ppermute | solution.py:27
  14.7 1.2 %copy-start.4 = (bf16[513,1024]{1,0:T(8,128)(2,1)S(1)}, bf16[513,1024]{1,0:T(8,128)(2,1)}, u32[]{:S(2)}) copy-start(bf16[513,1024]{1,0:T(8,128)(2,1)} %psi_ref) | copy-start | bytes 3151876
  17.9 8.9 %copy-start.5 = (f32[1024,64]{0,1:T(8,128)S(1)}, f32[1024,64]{0,1:T(8,128)}, u32[]{:S(2)}) copy-start(f32[1024,64]{0,1:T(8,128)} %param.13) | copy-start | bytes 786436
  18.0 8.9 %copy-start.6 = (f32[64,1024]{1,0:T(8,128)S(1)}, f32[64,1024]{1,0:T(8,128)}, u32[]{:S(2)}) copy-start(f32[64,1024]{1,0:T(8,128)} %get-tuple-element.41.own_ref) | copy-start | bytes 786436
  18.0 4.9 %collective-permute-start.4 = (f32[1,520,128]{2,1,0:T(8,128)S(1)}, f32[1,520,128]{2,1,0:T(8,128)S(1)}, u32[]{:S(2)}, u32[]{:S(2)}) collective-permute-start(f32[1,520,128]{2,1,0:T(8,128)S(1)} %get-tuple-element.32), channel_id=1, source_target_pairs={{0,4},{4,0},{8,12},{12,8},{16,20},{20,16},{24,28},{28,24},{1,5},{5... | collective-permute-start | bytes 798728 | tf_op jit(solution)/shard_map/ppermute | solution.py:27
  21.0 3.6 %collective-permute-start.9 = (f32[1,520,128]{2,1,0:T(8,128)S(1)}, f32[1,520,128]{2,1,0:T(8,128)S(1)}, u32[]{:S(2)}, u32[]{:S(2)}) collective-permute-start(f32[1,520,128]{2,1,0:T(8,128)S(1)} %get-tuple-element.33), channel_id=1, source_target_pairs={{0,4},{4,0},{8,12},{12,8},{16,20},{20,16},{24,28},{28,24},{1,5},{5... | collective-permute-start | bytes 798728 | tf_op jit(solution)/shard_map/ppermute | solution.py:27
  22.3 3.9 %collective-permute-start.11 = (f32[1,520,128]{2,1,0:T(8,128)S(1)}, f32[1,520,128]{2,1,0:T(8,128)S(1)}, u32[]{:S(2)}, u32[]{:S(2)}) collective-permute-start(f32[1,520,128]{2,1,0:T(8,128)S(1)} %get-tuple-element.34), channel_id=1, source_target_pairs={{0,4},{4,0},{8,12},{12,8},{16,20},{20,16},{24,28},{28,24},{1,5},{5... | collective-permute-start | bytes 798728 | tf_op jit(solution)/shard_map/ppermute | solution.py:27
  22.3 8.7 %collective-permute-start.13 = (f32[1,520,128]{2,1,0:T(8,128)S(1)}, f32[1,520,128]{2,1,0:T(8,128)S(1)}, u32[]{:S(2)}, u32[]{:S(2)}) collective-permute-start(f32[1,520,128]{2,1,0:T(8,128)S(1)} %get-tuple-element.35), channel_id=1, source_target_pairs={{0,4},{4,0},{8,12},{12,8},{16,20},{20,16},{24,28},{28,24},{1,5},{5... | collective-permute-start | bytes 798728 | tf_op jit(solution)/shard_map/ppermute | solution.py:27
  22.9 5.5 %collective-permute-start.6 = (f32[1,64,512]{2,1,0:T(8,128)S(1)}, f32[1,64,512]{2,1,0:T(8,128)S(1)}, u32[]{:S(2)}, u32[]{:S(2)}) collective-permute-start(f32[1,64,512]{2,1,0:T(8,128)S(1)} %add_add_fusion), channel_id=1, source_target_pairs={{0,1},{1,0},{2,3},{3,2},{4,5},{5,4},{6,7},{7,6},{8,9},{9,8},{10,11... | collective-permute-start | bytes 393224 | tf_op jit(solution)/shard_map/ppermute | solution.py:27
  24.6 13.9 %collective-permute-start.10 = (f32[1,520,128]{2,1,0:T(8,128)S(1)}, f32[1,520,128]{2,1,0:T(8,128)S(1)}, u32[]{:S(2)}, u32[]{:S(2)}) collective-permute-start(f32[1,520,128]{2,1,0:T(8,128)S(1)} %add.101), channel_id=1, source_target_pairs={{0,8},{4,12},{8,0},{12,4},{16,24},{20,28},{24,16},{28,20},{1,9},{5... | collective-permute-start | bytes 798728 | tf_op jit(solution)/shard_map/ppermute | solution.py:27
  26.2 15.2 %collective-permute-start.12 = (f32[1,520,128]{2,1,0:T(8,128)S(1)}, f32[1,520,128]{2,1,0:T(8,128)S(1)}, u32[]{:S(2)}, u32[]{:S(2)}) collective-permute-start(f32[1,520,128]{2,1,0:T(8,128)S(1)} %add.102), channel_id=1, source_target_pairs={{0,16},{4,20},{8,24},{12,28},{16,0},{20,4},{24,8},{28,12},{1,17},{... | collective-permute-start | bytes 798728 | tf_op jit(solution)/shard_map/ppermute | solution.py:27
  26.8 9.9 %copy-start.2 = (f32[1,64,1024]{2,1,0:T(8,128)S(1)}, f32[1,64,1024]{2,1,0:T(8,128)}, u32[]{:S(2)}) copy-start(f32[1,64,1024]{2,1,0:T(8,128)} %get-tuple-element.45.far_ref) | copy-start | bytes 786436
  26.9 14.7 %copy-start.1 = (f32[513,128]{1,0:T(8,128)S(1)}, f32[513,128]{1,0:T(8,128)}, u32[]{:S(2)}) copy-start(f32[513,128]{1,0:T(8,128)} %old_ref.1) | copy-start | bytes 787972
  28.4 8.3 %collective-permute-start.7 = (f32[1,64,512]{2,1,0:T(8,128)S(1)}, f32[1,64,512]{2,1,0:T(8,128)S(1)}, u32[]{:S(2)}, u32[]{:S(2)}) collective-permute-start(f32[1,64,512]{2,1,0:T(8,128)S(1)} %add.98), channel_id=1, source_target_pairs={{0,2},{1,3},{2,0},{3,1},{4,6},{5,7},{6,4},{7,5},{8,10},{9,11},{10,... | collective-permute-start | bytes 393224 | tf_op jit(solution)/shard_map/ppermute | solution.py:27
  31.1 20.2 %copy-start = (f32[512,512]{1,0:T(8,128)S(1)}, f32[512,512]{1,0:T(8,128)}, u32[]{:S(2)}) copy-start(f32[512,512]{1,0:T(8,128)} %old_ref.2) | copy-start | bytes 3145732
  31.1 10.4 %collective-permute-start.14 = (f32[1,520,128]{2,1,0:T(8,128)S(1)}, f32[1,520,128]{2,1,0:T(8,128)S(1)}, u32[]{:S(2)}, u32[]{:S(2)}) collective-permute-start(f32[1,520,128]{2,1,0:T(8,128)S(1)} %add.103), channel_id=1, source_target_pairs={{0,24},{4,28},{8,16},{12,20},{16,8},{20,12},{24,0},{28,4},{1,25},{... | collective-permute-start | bytes 798728 | tf_op jit(solution)/shard_map/ppermute | solution.py:27
  36.8 13.7 %collective-permute-start.8 = (f32[1,64,1024]{2,1,0:T(8,128)S(1)}, f32[1,64,1024]{2,1,0:T(8,128)S(1)}, u32[]{:S(2)}, u32[]{:S(2)}) collective-permute-start(f32[1,64,1024]{2,1,0:T(8,128)S(1)} %far_add.1), channel_id=1, source_target_pairs={{0,2},{1,3},{2,0},{3,1},{4,6},{5,7},{6,4},{7,5},{8,10},{9,11},{10,... | collective-permute-start | bytes 786440 | tf_op jit(solution)/shard_map/ppermute | solution.py:27
  37.1 6.6 %collective-permute-start.17 = (f32[1,64,512]{2,1,0:T(8,128)S(1)}, f32[1,64,512]{2,1,0:T(8,128)S(1)}, u32[]{:S(2)}, u32[]{:S(2)}) collective-permute-start(f32[1,64,512]{2,1,0:T(8,128)S(1)} %add.99.refs_0_), channel_id=1, source_target_pairs={{0,24},{4,28},{8,16},{12,20},{16,8},{20,12},{24,0},{28,4},{1,25},{... | collective-permute-start | bytes 393224 | tf_op jit(solution)/shard_map/ppermute | solution.py:27
  38.5 6.9 %collective-permute-start.16 = (f32[1,64,512]{2,1,0:T(8,128)S(1)}, f32[1,64,512]{2,1,0:T(8,128)S(1)}, u32[]{:S(2)}, u32[]{:S(2)}) collective-permute-start(f32[1,64,512]{2,1,0:T(8,128)S(1)} %add.99.refs_0_), channel_id=1, source_target_pairs={{0,16},{4,20},{8,24},{12,28},{16,0},{20,4},{24,8},{28,12},{1,17},{... | collective-permute-start | bytes 393224 | tf_op jit(solution)/shard_map/ppermute | solution.py:27
  41.4 5.0 %collective-permute-start.15 = (f32[1,64,512]{2,1,0:T(8,128)S(1)}, f32[1,64,512]{2,1,0:T(8,128)S(1)}, u32[]{:S(2)}, u32[]{:S(2)}) collective-permute-start(f32[1,64,512]{2,1,0:T(8,128)S(1)} %add.99.refs_0_), channel_id=1, source_target_pairs={{0,8},{4,12},{8,0},{12,4},{16,24},{20,28},{24,16},{28,20},{1,9},{5... | collective-permute-start | bytes 393224 | tf_op jit(solution)/shard_map/ppermute | solution.py:27
  41.5 9.7 %collective-permute-start.18 = (f32[1,64,512]{2,1,0:T(8,128)S(1)}, f32[1,64,512]{2,1,0:T(8,128)S(1)}, u32[]{:S(2)}, u32[]{:S(2)}) collective-permute-start(f32[1,64,512]{2,1,0:T(8,128)S(1)} %add.99.refs_0_), channel_id=1, source_target_pairs={{0,4},{4,0},{8,12},{12,8},{16,20},{20,16},{24,28},{28,24},{1,5},{5... | collective-permute-start | bytes 393224 | tf_op jit(solution)/shard_map/ppermute | solution.py:27
  46.4 4.9 %collective-permute-start.19 = (f32[1,64,512]{2,1,0:T(8,128)S(1)}, f32[1,64,512]{2,1,0:T(8,128)S(1)}, u32[]{:S(2)}, u32[]{:S(2)}) collective-permute-start(f32[1,64,512]{2,1,0:T(8,128)S(1)} %collective-permute-done.15.refs_1_), channel_id=1, source_target_pairs={{0,4},{4,0},{8,12},{12,8},{16,20},{20,16},{24,28},{28,24},{1,5},{5... | collective-permute-start | bytes 393224 | tf_op jit(solution)/shard_map/ppermute | solution.py:27
  46.4 4.9 %collective-permute-start.20 = (f32[1,64,512]{2,1,0:T(8,128)S(1)}, f32[1,64,512]{2,1,0:T(8,128)S(1)}, u32[]{:S(2)}, u32[]{:S(2)}) collective-permute-start(f32[1,64,512]{2,1,0:T(8,128)S(1)} %collective-permute-done.16.refs_2_), channel_id=1, source_target_pairs={{0,4},{4,0},{8,12},{12,8},{16,20},{20,16},{24,28},{28,24},{1,5},{5... | collective-permute-start | bytes 393224 | tf_op jit(solution)/shard_map/ppermute | solution.py:27
  46.9 4.4 %collective-permute-start.21 = (f32[1,64,512]{2,1,0:T(8,128)S(1)}, f32[1,64,512]{2,1,0:T(8,128)S(1)}, u32[]{:S(2)}, u32[]{:S(2)}) collective-permute-start(f32[1,64,512]{2,1,0:T(8,128)S(1)} %collective-permute-done.17.refs_3_), channel_id=1, source_target_pairs={{0,4},{4,0},{8,12},{12,8},{16,20},{20,16},{24,28},{28,24},{1,5},{5... | collective-permute-start | bytes 393224 | tf_op jit(solution)/shard_map/ppermute | solution.py:27
